TPU v7x, 32 devices: a whole 2x2x4 slice. The times are simulated.
32 devices in a mesh: req: 16 (over z, x, core), tp: 2 (over y).
Axes of the slice: x: 2, y: 2, z: 4, core: 2. Of those that a mesh axis runs over, the one named last changes fastest.
Arguments:
- queries: bfloat16 [4, 128, 1024], P(None, 'req', 'tp'), may hold values from -6 to 6
- new_kv: bfloat16 [4, 128, 2, 1024], P(None, 'req', None, 'tp'), may hold values from -4 to 4
- residual: bfloat16 [4, 128, 2048], P(None, 'req'), may hold values from -1.1953125 to 1.1953125
- home_cache: bfloat16 [64, 128, 2, 1024], P('req', None, None, 'tp'), may hold values from -6 to 6
- prompt_cache: bfloat16 [64, 128, 2, 1024], P('req', None, None, 'tp'), may hold values from -6 to 6
- home_table: int32 [128, 4], P('req'), may hold values from 0 to 3
- home_len: int32 [128], P('req'), may hold values from 1 to 512, as said below
- parents: int32 [4, 128], P(None, 'req'), may hold values from 0 to 7
- prompt_place: int32 [16], P('req'), may hold values from 0 to 15, as said below
- owned_request: int32 [16], P('req'), may hold values from 0 to 15, as said below
- prompt_len: int32 [16], P('req'), may hold values from 1 to 512, as said below
- out_weight: bfloat16 [1024, 2048], P('tp'), may hold values from -0.1875 to 0.1875
- norm_gain: bfloat16 [2048], replicated, may hold values from 0.099609375 to 1.8984375
- qkv_weight: bfloat16 [2048, 3, 1024], P(None, None, 'tp'), may hold values from -0.03125 to 0.03125
Outputs:
- next_qkv: bfloat16 [4, 128, 3, 1024], P(None, 'req', None, 'tp')
- new_residual: bfloat16 [4, 128, 2048], P(None, 'req')
Inputs may be any that keep to these rules, and one draw needn't show every extreme that they name: `home_len`: some beam has all 512 tokens. `prompt_len`: some prompt has all 512 tokens. `prompt_place`: A permutation. Slot j lies on device j. The 1 request of one device have their prompts on 1 different devices, each device holds prompts of 1 request of different devices, and a request's position among its device's requests equals its slot's position j % 1. `owned_request`: the inverse permutation of prompt_place.
All inputs are finite; a program needn't handle non-finite values.
Results may differ from a plain program's by a relative error of at most 0.013.
Values may be sent and summed in bfloat16 or wider, within the bound.
A program may use at most 128 MiB of HBM per device.

v0:
```python
import math

import jax
import jax.numpy as jnp
from jax import lax
from jax.sharding import PartitionSpec as P

HEAD_DIM = 64
BEAMS = 8


NEG_FILL = -1e30
NORM_EPS = 1e-05


def shards(
    queries,
    new_kv,
    residual,
    home_cache,
    prompt_cache,
    home_table,
    home_len,
    parents,
    prompt_place,
    owned_request,
    prompt_len,
    out_weight,
    norm_gain,
    qkv_weight,
):
    step_count, row_count, lane_count = queries.shape
    head_count = lane_count // HEAD_DIM
    request_count = row_count // BEAMS
    block_count = home_table.shape[1]
    block_size = home_cache.shape[1]
    prompt_tokens = prompt_cache.shape[0] * block_size // request_count
    home_tokens = block_count * block_size
    req_size = lax.axis_size("req")
    score_scale = 1.0 / math.sqrt(HEAD_DIM)
    request_base = jnp.arange(row_count, dtype=jnp.int32) // BEAMS * BEAMS
    first_parent = request_base + parents[0]
    tables = home_table[first_parent]
    lengths = home_len[first_parent]
    window = jnp.zeros((row_count, step_count, 2, lane_count), jnp.bfloat16)
    prompt_heads = prompt_cache.reshape(request_count, prompt_tokens, 2, head_count, HEAD_DIM)
    prompt_pos = jnp.arange(prompt_tokens, dtype=jnp.int32)
    home_pos = jnp.arange(home_tokens, dtype=jnp.int32)
    window_pos = jnp.arange(step_count, dtype=jnp.int32)
    gain_row = norm_gain.astype(jnp.float32)
    weight_flat = qkv_weight.reshape(qkv_weight.shape[0], 3 * lane_count)
    qkv_list = []
    residual_list = []
    for step_index in range(step_count):
        if step_index > 0:
            window = window.at[:, step_index - 1].set(new_kv[step_index - 1])
            chosen = request_base + parents[step_index]
            window = window[chosen]
            tables = tables[chosen]
            lengths = lengths[chosen]
        query_block = queries[step_index : step_index + 1]
        route_block_steps = query_block.shape[0]
        all_queries = lax.all_gather(query_block, "req", axis=1, tiled=True)
        route_query_held = all_queries.reshape(
            route_block_steps, req_size * request_count, BEAMS, head_count, HEAD_DIM
        )[:, owned_request]
        prompt_block_steps = route_query_held.shape[0]
        scores = (
            jnp.einsum(
                "krbhd,rthd->krbht",
                route_query_held,
                prompt_heads[:, :, 0],
                preferred_element_type=jnp.float32,
            )
            * score_scale
        )
        scores = jnp.where(
            prompt_pos[None, None, None, None, :] < prompt_len[None, :, None, None, None],
            scores,
            NEG_FILL,
        )
        row_top = jnp.max(scores, axis=-1)
        weights = jnp.exp(scores - row_top[..., None]).astype(jnp.bfloat16)
        weight_sum = jnp.sum(weights.astype(jnp.float32), axis=-1)
        numerator = jnp.einsum(
            "krbht,rthd->krbhd", weights, prompt_heads[:, :, 1], preferred_element_type=jnp.float32
        )
        held_numer = numerator.reshape(prompt_block_steps, row_count, lane_count)
        held_top = row_top.reshape(prompt_block_steps, row_count, head_count)
        held_sum = weight_sum.reshape(prompt_block_steps, row_count, head_count)
        all_numer = lax.all_gather(held_numer, "req", axis=1, tiled=True)
        all_top = lax.all_gather(held_top, "req", axis=1, tiled=True)
        all_sum_rows = lax.all_gather(held_sum, "req", axis=1, tiled=True)
        route_prompt_numer = all_numer.reshape(
            route_block_steps, req_size * request_count, BEAMS, lane_count
        )[:, prompt_place].reshape(route_block_steps, row_count, lane_count)
        route_prompt_top = all_top.reshape(
            route_block_steps, req_size * request_count, BEAMS, head_count
        )[:, prompt_place].reshape(route_block_steps, row_count, head_count)
        route_prompt_sum = all_sum_rows.reshape(
            route_block_steps, req_size * request_count, BEAMS, head_count
        )[:, prompt_place].reshape(route_block_steps, row_count, head_count)
        attend_prompt_numer = route_prompt_numer[0]
        attend_prompt_top = route_prompt_top[0]
        attend_prompt_sum = route_prompt_sum[0]
        query_heads = queries[step_index].reshape(row_count, head_count, HEAD_DIM)
        gathered = home_cache[tables].reshape(row_count, home_tokens, 2, head_count, HEAD_DIM)
        window_heads = window.reshape(row_count, step_count, 2, head_count, HEAD_DIM)
        own_heads = new_kv[step_index].reshape(row_count, 2, head_count, HEAD_DIM)
        home_scores = (
            jnp.einsum(
                "bhd,bthd->bht", query_heads, gathered[:, :, 0], preferred_element_type=jnp.float32
            )
            * score_scale
        )
        home_scores = jnp.where(
            home_pos[None, None, :] < lengths[:, None, None], home_scores, NEG_FILL
        )
        window_scores = (
            jnp.einsum(
                "bhd,bthd->bht",
                query_heads,
                window_heads[:, :, 0],
                preferred_element_type=jnp.float32,
            )
            * score_scale
        )
        window_scores = jnp.where(window_pos < step_index, window_scores, NEG_FILL)
        own_scores = (
            jnp.einsum(
                "bhd,bhd->bh", query_heads, own_heads[:, 0], preferred_element_type=jnp.float32
            )
            * score_scale
        )
        home_top = jnp.maximum(
            jnp.maximum(jnp.max(home_scores, axis=-1), jnp.max(window_scores, axis=-1)), own_scores
        )
        home_weights = jnp.exp(home_scores - home_top[..., None]).astype(jnp.bfloat16)
        window_weights = jnp.exp(window_scores - home_top[..., None]).astype(jnp.bfloat16)
        own_weights = jnp.exp(own_scores - home_top).astype(jnp.bfloat16)
        home_sum = (
            jnp.sum(home_weights.astype(jnp.float32), axis=-1)
            + jnp.sum(window_weights.astype(jnp.float32), axis=-1)
            + own_weights.astype(jnp.float32)
        )
        home_numer = jnp.einsum(
            "bht,bthd->bhd", home_weights, gathered[:, :, 1], preferred_element_type=jnp.float32
        )
        home_numer = home_numer + jnp.einsum(
            "bht,bthd->bhd",
            window_weights,
            window_heads[:, :, 1],
            preferred_element_type=jnp.float32,
        )
        home_numer = home_numer + own_weights.astype(jnp.float32)[..., None] * own_heads[
            :, 1
        ].astype(jnp.float32)
        attend_prompt_numer = attend_prompt_numer.reshape(row_count, head_count, HEAD_DIM)
        joint_top = jnp.maximum(home_top, attend_prompt_top)
        home_factor = jnp.exp(home_top - joint_top)
        prompt_factor = jnp.exp(attend_prompt_top - joint_top)
        joint_sum = home_sum * home_factor + attend_prompt_sum * prompt_factor
        joint_numer = (
            home_numer * home_factor[..., None] + attend_prompt_numer * prompt_factor[..., None]
        )
        attended = (
            (joint_numer / joint_sum[..., None]).astype(jnp.bfloat16).reshape(row_count, lane_count)
        )
        attended_block = attended[None]
        residual_block = residual[step_index : step_index + 1]
        block_steps = attended_block.shape[0]
        flat_rows = block_steps * row_count
        attended_flat = attended_block.reshape(flat_rows, lane_count)
        residual_flat = residual_block.reshape(flat_rows, residual_block.shape[-1])
        projected = jnp.dot(attended_flat, out_weight, preferred_element_type=jnp.float32)
        head_total = lax.psum(projected, "tp")
        mixed_rows = residual_flat.astype(jnp.float32) + head_total
        mean_square = jnp.mean(mixed_rows * mixed_rows, axis=-1, keepdims=True)
        normed = (mixed_rows * lax.rsqrt(mean_square + NORM_EPS) * gain_row).astype(jnp.bfloat16)
        residual_out = mixed_rows.astype(jnp.bfloat16)
        next_rows = jnp.dot(normed, weight_flat, preferred_element_type=jnp.float32).astype(
            jnp.bfloat16
        )
        qkv_step = next_rows.reshape(block_steps, row_count, 3, lane_count)
        residual_step = residual_out.reshape(block_steps, row_count, residual_out.shape[-1])
        qkv_list.append(qkv_step[0])
        residual_list.append(residual_step[0])
    return (jnp.stack(qkv_list), jnp.stack(residual_list))


def solution(mesh):
    placed = (
        P(None, "req", "tp"),
        P(None, "req", None, "tp"),
        P(None, "req", None),
        P("req", None, None, "tp"),
        P("req", None, None, "tp"),
        P("req", None),
        P("req"),
        P(None, "req"),
        P("req"),
        P("req"),
        P("req"),
        P("tp", None),
        P(),
        P(None, None, "tp"),
    )
    return jax.shard_map(
        shards,
        mesh=mesh,
        in_specs=placed,
        out_specs=(P(None, "req", None, "tp"), P(None, "req", None)),
        check_vma=False,
    )
```

profile of v0, /device:TPU:0, one launch (start us, length us, event | category | flops | bytes accessed | tf_op | source)
XLA Modules:
  0.0 679.1 jit_solution(5093690324050152967)
XLA Ops:
  7.8 1.4 fusion.151
  14.8 19.3 %gather_fusion.9 = bf16[32,128,2,512]{3,2,1,0:T(2,128)(2,1)} fusion(bf16[4,128,2,512]{3,2,1,0:T(2,128)(2,1)} %param.23, s32[1024]{0:T(1024)S(1)} %pad_clamp_fusion.2), kind=kCustom, calls=%fused_computation.9 | custom fusion | bytes 16777344 | tf_op jit(solution)/shard_map/gather | solution.py:107
  34.1 14.6 %copy.185 = bf16[32,128,2,512]{1,0,3,2:T(8,128)(2,1)} copy(bf16[32,128,2,512]{3,2,1,0:T(2,128)(2,1)} %gather_fusion.9) | data formatting | bytes 16777216 | tf_op jit(solution)/shard_map/gather | solution.py:107
  48.7 13.9 %reshape.675 = bf16[8,512,2,8,64]{1,0,4,3,2:T(8,128)(2,1)} reshape(bf16[32,128,2,512]{1,0,3,2:T(8,128)(2,1)} %copy.185) | data formatting | bytes 16777216 | tf_op jit(solution)/shard_map/reshape | solution.py:107
  62.6 5.8 slice_bitcast_fusion.3
  73.4 4.5 fusion.6
  81.6 2.0 convert_reduce_fusion.3
  83.6 1.9 convert_reduce_fusion.9
  85.5 23.7 %all_gather.56 = bf16[1,128,512]{2,1,0:T(8,128)(2,1)S(1)} all-gather(bf16[1,8,512]{2,1,0:T(8,128)(2,1)} %copy-done.16), channel_id=1, replica_groups=mesh['req'=16,'tp'=2] {'req'}, dimensions={1}, use_global_device_ids=true | all-gather | bytes 139264 | tf_op jit(solution)/shard_map/all_gather | solution.py:63
  111.4 18.5 %all_gather.60 = bf16[1,128,512]{2,1,0:T(8,128)(2,1)S(1)} all-gather(bf16[1,8,512]{2,1,0:T(8,128)(2,1)} %get-tuple-element.273), channel_id=1, replica_groups=mesh['req'=16,'tp'=2] {'req'}, dimensions={1}, use_global_device_ids=true | all-gather | bytes 139264 | tf_op jit(solution)/shard_map/all_gather | solution.py:63
  130.8 3.8 copy.167
  134.7 2.3 reshape.652
  137.6 1.3 constant_dynamic-slice_fusion.3
  141.7 2.0 convolution_bitcast_fusion.1
  143.7 1.4 reshape.1306
  147.1 1.4 reshape_squeeze.30
  149.3 18.1 %gather_fusion.13 = bf16[32,128,2,512]{3,2,1,0:T(2,128)(2,1)} fusion(bf16[4,128,2,512]{3,2,1,0:T(2,128)(2,1)S(1)} %copy-done.1, s32[1024]{0:T(1024)S(1)} %pad_clamp_fusion), kind=kCustom, calls=%fused_computation.13 | custom fusion | bytes 16777344 | tf_op jit(solution)/shard_map/gather | solution.py:107
  167.4 14.6 %copy.194 = bf16[32,128,2,512]{1,0,3,2:T(8,128)(2,1)} copy(bf16[32,128,2,512]{3,2,1,0:T(2,128)(2,1)} %gather_fusion.13) | data formatting | bytes 16777216 | tf_op jit(solution)/shard_map/gather | solution.py:107
  182.1 13.9 %reshape.687 = bf16[8,512,2,8,64]{1,0,4,3,2:T(8,128)(2,1)} reshape(bf16[32,128,2,512]{1,0,3,2:T(8,128)(2,1)} %copy.194) | data formatting | bytes 16777216 | tf_op jit(solution)/shard_map/reshape | solution.py:107
  196.0 5.8 slice_bitcast_fusion.1
  202.4 1.4 gather_fusion.14
  205.5 4.6 fusion.2
  213.5 1.9 convert_reduce_fusion.8
  218.1 2.0 convolution_bitcast_fusion
  221.9 18.1 %gather_fusion.5 = bf16[32,128,2,512]{3,2,1,0:T(2,128)(2,1)} fusion(bf16[4,128,2,512]{3,2,1,0:T(2,128)(2,1)S(1)} %copy-done.1, s32[1024]{0:T(1024)S(1)} %pad_clamp_fusion.4), kind=kCustom, calls=%fused_computation.5 | custom fusion | bytes 16777344 | tf_op jit(solution)/shard_map/gather | solution.py:107
  240.0 14.6 %copy.176 = bf16[32,128,2,512]{1,0,3,2:T(8,128)(2,1)} copy(bf16[32,128,2,512]{3,2,1,0:T(2,128)(2,1)} %gather_fusion.5) | data formatting | bytes 16777216 | tf_op jit(solution)/shard_map/gather | solution.py:107
  254.6 14.0 %reshape.663 = bf16[8,512,2,8,64]{1,0,4,3,2:T(8,128)(2,1)} reshape(bf16[32,128,2,512]{1,0,3,2:T(8,128)(2,1)} %copy.176) | data formatting | bytes 16777216 | tf_op jit(solution)/shard_map/reshape | solution.py:107
  268.6 5.2 slice_bitcast_fusion.5
  273.8 2.4 fusion.10
  277.0 1.3 convert_reduce_fusion.5
  279.5 19.2 %all_gather.52 = bf16[1,128,512]{2,1,0:T(8,128)(2,1)S(1)} all-gather(bf16[1,8,512]{2,1,0:T(8,128)(2,1)S(1)} %copy-done.15), channel_id=1, replica_groups=mesh['req'=16,'tp'=2] {'req'}, dimensions={1}, use_global_device_ids=true | all-gather | bytes 139264 | tf_op jit(solution)/shard_map/all_gather | solution.py:63
  298.8 17.8 %all_gather.48 = bf16[1,128,512]{2,1,0:T(8,128)(2,1)S(1)} all-gather(bf16[1,8,512]{2,1,0:T(8,128)(2,1)S(1)} %get-tuple-element.272), channel_id=1, replica_groups=mesh['req'=16,'tp'=2] {'req'}, dimensions={1}, use_global_device_ids=true | all-gather | bytes 139264 | tf_op jit(solution)/shard_map/all_gather | solution.py:63
  317.6 1.3 constant_dynamic-slice_fusion.11
  321.7 1.3 convolution_bitcast_fusion.2
  323.3 1.3 fusion.152
  324.8 1.3 convolution_bitcast_fusion.3
  327.0 18.9 %all-gather.5 = f32[128,8]{1,0:T(8,128)S(1)} all-gather(f32[8,8]{1,0:T(8,128)S(1)} %copy.189), channel_id=7, replica_groups=mesh['req'=16,'tp'=2] {'req'}, dimensions={0}, use_global_device_ids=true | all-gather | bytes 4352 | tf_op jit(solution)/shard_map/all_gather | solution.py:93
  345.9 17.9 %all-gather.4 = f32[128,8]{1,0:T(8,128)S(1)} all-gather(f32[8,8]{1,0:T(8,128)} %copy.187), channel_id=6, replica_groups=mesh['req'=16,'tp'=2] {'req'}, dimensions={0}, use_global_device_ids=true | all-gather | bytes 4352 | tf_op jit(solution)/shard_map/all_gather | solution.py:92
  363.7 1.4 copy.238
  366.0 19.4 %all_gather.58 = f32[1,128,512]{2,1,0:T(8,128)S(1)} all-gather(f32[1,8,512]{2,1,0:T(8,128)S(1)} %reshape.683), channel_id=1, replica_groups=mesh['req'=16,'tp'=2] {'req'}, dimensions={1}, use_global_device_ids=true | all-gather | bytes 278528 | tf_op jit(solution)/shard_map/all_gather | solution.py:91
  385.6 4.6 fusion.4
  391.4 17.7 %all-gather.7 = f32[128,8]{1,0:T(8,128)S(1)} all-gather(f32[8,8]{1,0:T(8,128)S(1)} %copy.198), channel_id=9, replica_groups=mesh['req'=16,'tp'=2] {'req'}, dimensions={0}, use_global_device_ids=true | all-gather | bytes 4352 | tf_op jit(solution)/shard_map/all_gather | solution.py:93
  409.1 19.1 %all-gather.6 = f32[128,8]{1,0:T(8,128)S(1)} all-gather(f32[8,8]{1,0:T(8,128)} %copy.196), channel_id=8, replica_groups=mesh['req'=16,'tp'=2] {'req'}, dimensions={0}, use_global_device_ids=true | all-gather | bytes 4352 | tf_op jit(solution)/shard_map/all_gather | solution.py:92
  429.0 18.2 %all_gather.62 = f32[1,128,512]{2,1,0:T(8,128)S(1)} all-gather(f32[1,8,512]{2,1,0:T(8,128)S(1)} %reshape.695), channel_id=1, replica_groups=mesh['req'=16,'tp'=2] {'req'}, dimensions={1}, use_global_device_ids=true | all-gather | bytes 278528 | tf_op jit(solution)/shard_map/all_gather | solution.py:91
  447.3 4.5 fusion
  454.5 18.9 %all-gather.3 = f32[128,8]{1,0:T(8,128)S(1)} all-gather(f32[8,8]{1,0:T(8,128)S(1)} %copy.180), channel_id=5, replica_groups=mesh['req'=16,'tp'=2] {'req'}, dimensions={0}, use_global_device_ids=true | all-gather | bytes 4352 | tf_op jit(solution)/shard_map/all_gather | solution.py:93
  473.3 17.9 %all-gather.2 = f32[128,8]{1,0:T(8,128)S(1)} all-gather(f32[8,8]{1,0:T(8,128)S(1)} %copy-done.47), channel_id=4, replica_groups=mesh['req'=16,'tp'=2] {'req'}, dimensions={0}, use_global_device_ids=true | all-gather | bytes 4352 | tf_op jit(solution)/shard_map/all_gather | solution.py:92
  492.0 19.4 %all_gather.54 = f32[1,128,512]{2,1,0:T(8,128)S(1)} all-gather(f32[1,8,512]{2,1,0:T(8,128)S(1)} %reshape.671), channel_id=1, replica_groups=mesh['req'=16,'tp'=2] {'req'}, dimensions={1}, use_global_device_ids=true | all-gather | bytes 278528 | tf_op jit(solution)/shard_map/all_gather | solution.py:91
  511.6 4.5 fusion.8
  517.8 18.3 %gather_fusion.2 = bf16[32,128,2,512]{3,2,1,0:T(2,128)(2,1)} fusion(bf16[4,128,2,512]{3,2,1,0:T(2,128)(2,1)S(1)} %copy-done.1, s32[1024]{0:T(1024)S(1)} %pad_clamp_fusion.6), kind=kCustom, calls=%fused_computation.2 | custom fusion | bytes 16777344 | tf_op jit(solution)/shard_map/gather | solution.py:107
  536.1 14.6 %copy.165 = bf16[32,128,2,512]{1,0,3,2:T(8,128)(2,1)} copy(bf16[32,128,2,512]{3,2,1,0:T(2,128)(2,1)} %gather_fusion.2) | data formatting | bytes 16777216 | tf_op jit(solution)/shard_map/gather | solution.py:107
  550.7 13.9 %reshape.649 = bf16[8,512,2,8,64]{1,0,4,3,2:T(8,128)(2,1)} reshape(bf16[32,128,2,512]{1,0,3,2:T(8,128)(2,1)} %copy.165) | data formatting | bytes 16777216 | tf_op jit(solution)/shard_map/reshape | solution.py:107
  564.6 5.7 slice_bitcast_fusion.7
  570.4 4.5 fusion.14
  575.4 17.6 %all-gather.1 = f32[128,8]{1,0:T(8,128)S(1)} all-gather(f32[8,8]{1,0:T(8,128)S(1)} %copy.170), channel_id=3, replica_groups=mesh['req'=16,'tp'=2] {'req'}, dimensions={0}, use_global_device_ids=true | all-gather | bytes 4352 | tf_op jit(solution)/shard_map/all_gather | solution.py:93
  593.0 18.9 %all-gather = f32[128,8]{1,0:T(8,128)S(1)} all-gather(f32[8,8]{1,0:T(8,128)S(1)} %copy.168), channel_id=2, replica_groups=mesh['req'=16,'tp'=2] {'req'}, dimensions={0}, use_global_device_ids=true | all-gather | bytes 4352 | tf_op jit(solution)/shard_map/all_gather | solution.py:92
  612.3 18.4 %all_gather.50 = f32[1,128,512]{2,1,0:T(8,128)S(1)} all-gather(f32[1,8,512]{2,1,0:T(8,128)S(1)} %reshape.658), channel_id=1, replica_groups=mesh['req'=16,'tp'=2] {'req'}, dimensions={1}, use_global_device_ids=true | all-gather | bytes 278528 | tf_op jit(solution)/shard_map/all_gather | solution.py:91
  630.8 4.5 fusion.12
  636.6 8.9 %copy.173 = bf16[2048,3,512]{0,2,1:T(8,128)(2,1)} copy(bf16[2048,3,512]{2,0,1:T(8,128)(2,1)} %param.33) | data formatting | bytes 12582912 | tf_op args[13]
  645.5 13.3 %all-reduce.4.cloned.1.call-done = (f32[8,2048]{1,0:T(8,128)}, f32[8,2048]{1,0:T(8,128)}, f32[8,2048]{1,0:T(8,128)}, f32[8,2048]{1,0:T(8,128)}) async-done(((f32[8,2048]{1,0:T(8,128)}, f32[8,2048]{1,0:T(8,128)}, f32[8,2048]{1,0:T(8,128)}, f32[8,2048]{1,0:T(8,128)}), (f32[8,2048]{1,0:T(8,128)}, f32[8,2048]{1,0:T(8,128)}, f32[8,2048]{1,0:T(8,128)}, f32[8,2048]{1,0:T(8,128)})) %all-reduce.4.cloned.1.call-update) | async-done | bytes 262160 | tf_op jit(solution)/shard_map/psum | solution.py:176
  660.1 5.1 convolution_convert_fusion.3
  665.2 1.7 convolution_convert_fusion.2
  667.0 1.7 convolution_convert_fusion.1
  668.7 1.7 convolution_convert_fusion
  (271 shorter events, 52.5 us)
Async XLA Ops:
  7.2 445.2 %copy-start = (bf16[512,2048]{1,0:T(8,128)(2,1)S(1)}, bf16[512,2048]{1,0:T(8,128)(2,1)}, u32[]{:S(2)}) copy-start(bf16[512,2048]{1,0:T(8,128)(2,1)} %param.31) | copy-start | bytes 6291460
  7.2 651.6 %all-reduce.4.cloned.1.call-start = ((), (), s32[]{:S(2)}) async-start(), calls=%async_computation | async-start | bytes 524288 | tf_op jit(solution)/shard_map/psum | solution.py:176
  9.2 1.6 copy-start.16
  9.3 64.2 %copy-start.41 = (bf16[8,8,64,1]{2,3,1,0:T(2,128)(2,1)}, bf16[8,8,64,1]{2,3,1,0:T(2,128)(2,1)S(1)}, u32[]{:S(2)}) copy-start(bf16[8,8,64,1]{2,3,1,0:T(2,128)(2,1)S(1)} %reshape.1304) | copy-start | bytes 24580
  11.6 1.8 copy-start.57
  62.6 5.8 copy-start.2
  62.6 7.8 %copy-start.8 = (bf16[4,8,2,512]{3,2,1,0:T(2,128)(2,1)S(1)}, bf16[4,8,2,512]{3,2,1,0:T(2,128)(2,1)}, u32[]{:S(2)}) copy-start(bf16[4,8,2,512]{3,2,1,0:T(2,128)(2,1)} %param.21) | copy-start | bytes 196612
  70.4 10.4 %copy-start.33 = (pred[8,512]{1,0:T(8,128)(4,1)}, pred[8,512]{1,0:T(8,128)(4,1)S(1)}, u32[]{:S(2)}) copy-start(pred[8,512]{1,0:T(8,128)(4,1)S(1)} %iota_compare_fusion.1) | copy-start | bytes 12292
  78.0 71.4 %copy-start.1 = (bf16[4,128,2,512]{3,2,1,0:T(2,128)(2,1)S(1)}, bf16[4,128,2,512]{3,2,1,0:T(2,128)(2,1)}, u32[]{:S(2)}) copy-start(bf16[4,128,2,512]{3,2,1,0:T(2,128)(2,1)} %param.23) | copy-start | bytes 3145732
  80.0 87.5 %copy-start.9 = (bf16[8,2,8,64]{3,2,1,0:T(8,128)(2,1)}, bf16[8,2,8,64]{3,2,1,0:T(8,128)(2,1)S(1)}, u32[]{:S(2)}) copy-start(bf16[8,2,8,64]{3,2,1,0:T(8,128)(2,1)S(1)} %reshape_squeeze.29) | copy-start | bytes 49156
  81.6 3.9 copy-start.35
  137.6 29.8 %copy-start.55 = (pred[512]{0:T(512)(128)(4,1)}, pred[512]{0:T(512)(128)(4,1)S(1)}, u32[]{:S(2)}) copy-start(pred[512]{0:T(512)(128)(4,1)S(1)} %iota_compare_fusion.4) | copy-start | bytes 1540
  201.8 9.4 %copy-start.22 = (bf16[1,8,2,512]{3,2,1,0:T(2,128)(2,1)S(1)}, bf16[1,8,2,512]{3,2,1,0:T(2,128)(2,1)}, u32[]{:S(2)}) copy-start(bf16[1,8,2,512]{3,2,1,0:T(2,128)(2,1)} %get-tuple-element.269) | copy-start | bytes 49156
  201.8 10.3 %copy-start.24 = (bf16[8,8,64]{2,1,0:T(8,128)(2,1)S(1)}, bf16[8,8,64]{2,1,0:T(8,128)(2,1)}, u32[]{:S(2)}) copy-start(bf16[8,8,64]{2,1,0:T(8,128)(2,1)} %reshape_squeeze.30) | copy-start | bytes 24580
  201.8 13.6 %copy-start.23 = (bf16[1,1,8,8,64]{4,3,2,1,0:T(8,128)(2,1)S(1)}, bf16[1,1,8,8,64]{4,3,2,1,0:T(8,128)(2,1)}, u32[]{:S(2)}) copy-start(bf16[1,1,8,8,64]{4,3,2,1,0:T(8,128)(2,1)} %get-tuple-element.292) | copy-start | bytes 24580
  203.9 7.4 %copy-start.34 = (pred[8,512]{1,0:T(8,128)(4,1)S(1)}, pred[8,512]{1,0:T(8,128)(4,1)}, u32[]{:S(2)}) copy-start(pred[8,512]{1,0:T(8,128)(4,1)} %iota_compare_fusion) | copy-start | bytes 12292
  205.5 15.5 %copy-start.15 = (bf16[1,8,512]{2,1,0:T(8,128)(2,1)S(1)}, bf16[1,8,512]{2,1,0:T(8,128)(2,1)}, u32[]{:S(2)}) copy-start(bf16[1,8,512]{2,1,0:T(8,128)(2,1)} %get-tuple-element.271) | copy-start | bytes 24580
  211.3 28.8 %copy-start.11 = (bf16[8,2,8,64]{3,2,1,0:T(8,128)(2,1)}, bf16[8,2,8,64]{3,2,1,0:T(8,128)(2,1)S(1)}, u32[]{:S(2)}) copy-start(bf16[8,2,8,64]{3,2,1,0:T(8,128)(2,1)S(1)} %reshape_squeeze.31) | copy-start | bytes 49156
  212.2 27.9 %copy-start.37 = (f32[8,8]{1,0:T(8,128)}, f32[8,8]{1,0:T(8,128)S(1)}, u32[]{:S(2)}) copy-start(f32[8,8]{1,0:T(8,128)S(1)} %fusion.72) | copy-start | bytes 772
  212.2 3.2 copy-start.29
  273.8 2.4 copy-start.28
  273.8 2.7 copy-start.21
  276.6 22.1 %copy-start.13 = (bf16[8,2,8,64]{3,2,1,0:T(8,128)(2,1)}, bf16[8,2,8,64]{3,2,1,0:T(8,128)(2,1)S(1)}, u32[]{:S(2)}) copy-start(bf16[8,2,8,64]{3,2,1,0:T(8,128)(2,1)S(1)} %reshape_squeeze.27) | copy-start | bytes 49156
  276.9 21.8 %copy-start.39 = (f32[8,8]{1,0:T(8,128)}, f32[8,8]{1,0:T(8,128)S(1)}, u32[]{:S(2)}) copy-start(f32[8,8]{1,0:T(8,128)S(1)} %fusion.74) | copy-start | bytes 772
  276.9 21.8 %copy-start.31 = (f32[8,8]{1,0:T(8,128)}, f32[8,8]{1,0:T(8,128)S(1)}, u32[]{:S(2)}) copy-start(f32[8,8]{1,0:T(8,128)S(1)} %maximum_maximum_fusion.2) | copy-start | bytes 772
  385.5 4.7 copy-start.25
  385.5 4.7 copy-start.42
  385.5 4.9 copy-start.36
  385.5 4.9 copy-start.49
  385.5 4.9 copy-start.52
  385.5 4.9 copy-start.10
  385.5 42.6 %copy-start.45 = (bf16[8,8,4,1]{1,0,2,3:T(8,128)(2,1)S(1)}, bf16[8,8,4,1]{1,0,2,3:T(8,128)(2,1)}, u32[]{:S(2)}) copy-start(bf16[8,8,4,1]{1,0,2,3:T(8,128)(2,1)} %get-tuple-element.277) | copy-start | bytes 1540
  385.5 43.4 %copy-start.17 = (f32[1,1,8,8,64]{4,2,3,0,1:T(8,128)S(1)}, f32[1,1,8,8,64]{4,2,3,0,1:T(8,128)}, u32[]{:S(2)}) copy-start(f32[1,1,8,8,64]{4,2,3,0,1:T(8,128)} %convolution_bitcast_fusion) | copy-start | bytes 49156
  385.5 61.7 %copy-start.18 = (bf16[8,8,512,1]{2,1,0,3:T(8,128)(2,1)S(1)}, bf16[8,8,512,1]{2,1,0,3:T(8,128)(2,1)}, u32[]{:S(2)}) copy-start(bf16[8,8,512,1]{2,1,0,3:T(8,128)(2,1)} %get-tuple-element.254) | copy-start | bytes 196612
  447.3 4.6 copy-start.27
  447.3 4.6 copy-start.43
  447.3 4.8 copy-start.30
  447.3 4.8 copy-start.38
  447.3 4.8 copy-start.50
  447.3 4.8 copy-start.53
  447.3 4.8 copy-start.12
  451.9 2.5 copy-start.48
  451.9 21.5 %copy-start.47 = (f32[8,8]{1,0:T(8,128)S(1)}, f32[8,8]{1,0:T(8,128)}, u32[]{:S(2)}) copy-start(f32[8,8]{1,0:T(8,128)} %copy.178) | copy-start | bytes 772
  451.9 39.3 %copy-start.46 = (bf16[8,8,4,1]{1,0,2,3:T(8,128)(2,1)S(1)}, bf16[8,8,4,1]{1,0,2,3:T(8,128)(2,1)}, u32[]{:S(2)}) copy-start(bf16[8,8,4,1]{1,0,2,3:T(8,128)(2,1)} %get-tuple-element.279) | copy-start | bytes 1540
  451.9 59.7 %copy-start.19 = (bf16[8,8,512,1]{2,1,0,3:T(8,128)(2,1)S(1)}, bf16[8,8,512,1]{2,1,0,3:T(8,128)(2,1)}, u32[]{:S(2)}) copy-start(bf16[8,8,512,1]{2,1,0,3:T(8,128)(2,1)} %get-tuple-element.256) | copy-start | bytes 196612
  511.5 4.6 copy-start.26
  511.5 4.6 copy-start.44
  511.5 4.8 copy-start.32
  511.5 4.8 copy-start.40
  511.5 4.8 copy-start.51
  511.6 4.8 copy-start.54
  511.6 4.8 copy-start.14
  511.6 6.1 copy-start.56
  564.6 5.7 copy-start.20
  636.6 8.9 %copy-start.58 = (bf16[2048]{0:T(1024)(128)(2,1)S(1)}, bf16[2048]{0:T(1024)(128)(2,1)}, u32[]{:S(2)}) copy-start(bf16[2048]{0:T(1024)(128)(2,1)} %param.32) | copy-start | bytes 12292
  636.6 22.2 %copy-start.4 = (bf16[4,8,2048]{2,1,0:T(8,128)(2,1)S(1)}, bf16[4,8,2048]{2,1,0:T(8,128)(2,1)}, u32[]{:S(2)}) copy-start(bf16[4,8,2048]{2,1,0:T(8,128)(2,1)} %param.22) | copy-start | bytes 393220
  658.8 6.4 copy-start.3
  658.8 6.4 copy-start.7
  665.2 1.8 copy-start.6
  667.0 1.8 copy-start.5
Sparse Core Ops, SparseCore 0:
  636.7 22.0 all-reduce.3
where the time goes:
time: 689 us; the launch traced here: 679 us
  blocking collectives  301 us (44%)
  local copies, waits for them, and re-layouts  261 us (38%)
  matrix products  63.4 us (9%)
  other arithmetic  22.4 us (3%)
  between operations  17.2 us (2%)
  waiting for transfers between devices  13.3 us (2%)
    gather x8, local copies, waits for them, and re-layouts, shards(): home_cache[tables].reshape(row_count, home_tokens, 2, head_count, HEAD_DIM)  132 us
    all_gather x4, blocking collectives, shards(): all_queries = lax.all_gather(query_block, 'req', axis=1, tiled=True)  79.2 us
    all_gather x4, blocking collectives, shards(): all_numer = lax.all_gather(held_numer, 'req', axis=1, tiled=True)  75.4 us
    all_gather x4, blocking collectives, shards(): all_top = lax.all_gather(held_top, 'req', axis=1, tiled=True)  73.7 us
    all_gather x4, blocking collectives, shards(): all_sum_rows = lax.all_gather(held_sum, 'req', axis=1, tiled=True)  73.1 us
    reshape x4, local copies, waits for them, and re-layouts, shards(): home_cache[tables].reshape(row_count, home_tokens, 2, head_count, HEAD_DIM)  55.7 us
    squeeze x4, local copies, waits for them, and re-layouts, shards(): gathered[:, :, 0]  22.5 us
    dot_general x4, matrix products, shards(): jnp.einsum('bht,bthd->bhd', home_weights, gathered[:, :, 1], preferred_el...  18.2 us
  transfers between devices with their start and end apart: 1, of which 1 were waited for; matrix products, arithmetic and copies ran while one was open for 1% of the time, Pallas kernels for 0%

commit v1 on v0

v1 whole, which is shorter than its diff:
```python
import functools
import math

import jax
import jax.numpy as jnp
from jax import lax
from jax.experimental import pallas as pl
from jax.experimental.pallas import tpu as pltpu
from jax.sharding import PartitionSpec as P

HEAD_DIM = 64
BEAMS = 8
LANES = 128
OUT_CHUNKS = 4

NEG_FILL = -1e30
NORM_EPS = 1e-05


def grid_of(req_size):
    chips = req_size // 2
    outer = 4 if chips % 4 == 0 else 1
    return outer, chips // outer


def spread_heads(q, heads):
    rows, lanes = q.shape
    scaled = q.astype(jnp.float32) * (1.0 / math.sqrt(HEAD_DIM))
    lane_head = lax.broadcasted_iota(jnp.int32, (rows, lanes), 1) // HEAD_DIM
    parts = [jnp.where(lane_head == h, scaled, 0.0) for h in range(heads)]
    return jnp.concatenate(parts, axis=0).astype(jnp.bfloat16)


def dot_t(a, b):
    return lax.dot_general(a, b, (((1,), (1,)), ((), ())), preferred_element_type=jnp.float32)


def own_columns(wide, rows, lanes):
    first = lax.broadcasted_iota(jnp.int32, (rows, LANES), 1) < HEAD_DIM
    tiles = []
    for t in range(lanes // LANES):
        cols = slice(t * LANES, (t + 1) * LANES)
        a = wide[2 * t * rows : (2 * t + 1) * rows, cols]
        b = wide[(2 * t + 1) * rows : (2 * t + 2) * rows, cols]
        tiles.append(jnp.where(first, a, b))
    return tiles[0] if len(tiles) == 1 else jnp.concatenate(tiles, axis=1)


def kernel(
    req_size, tp_size, steps,
    table_ref, len_ref, parents_ref, place_ref, owned_ref, plen_ref,
    q_ref, nk_ref, nv_ref, res_ref, gain_ref,
    hk_hbm, hv_hbm, pk_hbm, pv_hbm, wo_hbm, wq_hbm,
    qkv_out, res_out,
    qbuf, pbuf, obuf, hk, hv, pk, pv, wo, wq, base, acc,
    load_sem, qsend, qrecv, psend, precv, osend, orecv,
):
    rows, lanes = q_ref.shape
    heads = lanes // HEAD_DIM
    depth = res_ref.shape[1]
    chunk = depth // OUT_CHUNKS
    tokens = hk.shape[0]
    block_count = table_ref.shape[0]
    block = tokens // block_count
    outer, inner = grid_of(req_size)
    me = lax.axis_index("req")
    my_tp = lax.axis_index("tp")
    c = lax.rem(me, 2)
    i = lax.rem(me // 2, inner)
    o = me // (2 * inner)

    def at(oo, ii, cc):
        return (oo * inner + ii) * 2 + cc

    outer_peers = [at(lax.rem(o + d, outer), i, c) for d in range(1, outer)]
    inner_peers = [at(o, lax.rem(i + e, inner), c) for e in range(1, inner)]
    core_peer = at(o, i, 1 - c)
    tp_peers = [lax.rem(my_tp + d, tp_size) for d in range(1, tp_size)]

    barrier = pltpu.get_barrier_semaphore()
    for peer in outer_peers + inner_peers + [core_peer]:
        pl.semaphore_signal(barrier, inc=1, device_id={"req": peer}, device_id_type=pl.DeviceIdType.MESH)
    for peer in tp_peers:
        pl.semaphore_signal(barrier, inc=1, device_id={"tp": peer}, device_id_type=pl.DeviceIdType.MESH)

    loads = [
        pltpu.make_async_copy(src, dst, load_sem.at[n])
        for n, (src, dst) in enumerate(
            [(pk_hbm, pk), (pv_hbm, pv), (hk_hbm, hk), (hv_hbm, hv), (wo_hbm, wo), (wq_hbm, wq)]
        )
    ]
    for copy in loads:
        copy.start()
    qbuf[me] = q_ref[...]

    pl.semaphore_wait(barrier, len(outer_peers) + len(inner_peers) + 1 + len(tp_peers))

    def gather(buf, send, recv, between):
        sent = []

        def push(slot, peer):
            copy = pltpu.make_async_remote_copy(
                src_ref=buf.at[slot], dst_ref=buf.at[slot],
                send_sem=send.at[len(sent)], recv_sem=recv.at[slot],
                device_id={"req": peer}, device_id_type=pl.DeviceIdType.MESH,
            )
            copy.start()
            sent.append(copy)

        def arrive(slot):
            pltpu.make_async_remote_copy(
                src_ref=buf.at[slot], dst_ref=buf.at[slot],
                send_sem=send.at[0], recv_sem=recv.at[slot],
                device_id={"req": core_peer}, device_id_type=pl.DeviceIdType.MESH,
            ).wait_recv()

        for peer in reversed(outer_peers):
            push(me, peer)
        for peer in inner_peers + [core_peer]:
            push(me, peer)
        result = between()
        for d in range(1, outer):
            slot = at(lax.rem(o + d, outer), i, c)
            arrive(slot)
            for peer in inner_peers + [core_peer]:
                push(slot, peer)
        for e in range(1, inner):
            for d in range(outer):
                slot = at(lax.rem(o + d, outer), lax.rem(i + e, inner), c)
                arrive(slot)
                push(slot, core_peer)
        for e in range(inner):
            for d in range(outer):
                arrive(at(lax.rem(o + d, outer), lax.rem(i + e, inner), 1 - c))
        return result, sent

    def key_counts():
        lane = lax.broadcasted_iota(jnp.int32, (1, tokens), 1)
        lane_block = lane // block
        lane_pos = lane - lane_block * block
        for p in range(BEAMS):
            total = jnp.zeros((1, tokens), jnp.float32)
            for j in range(block_count):
                live = (lane_block == table_ref[j, p]) & (lane_pos + j * block < len_ref[p])
                total = total + jnp.where(live, 1.0, 0.0)
            base[p : p + 1, :] = total
        pool = base[...]
        row8 = lax.broadcasted_iota(jnp.int32, (BEAMS, BEAMS), 0)
        col8 = lax.broadcasted_iota(jnp.int32, (BEAMS, BEAMS), 1)
        new_row = lax.broadcasted_iota(jnp.int32, (BEAMS, rows), 0)
        new_col = lax.broadcasted_iota(jnp.int32, (BEAMS, rows), 1)
        new = jnp.zeros((BEAMS, rows), jnp.float32)
        pools, news = [], []
        for s in range(steps):
            pick = jnp.zeros((BEAMS, BEAMS), jnp.float32)
            for b in range(BEAMS):
                pick = jnp.where((row8 == b) & (col8 == parents_ref[s, b]), 1.0, pick)
            pool = jnp.dot(pick, pool, preferred_element_type=jnp.float32)
            new = jnp.dot(pick, new, preferred_element_type=jnp.float32)
            new = new + jnp.where(new_col == new_row + s * BEAMS, 1.0, 0.0)
            pools.append(pool)
            news.append(new)
        return jnp.concatenate(pools, axis=0), jnp.concatenate(news, axis=0)

    (pool_count, new_count), q_sent = gather(qbuf, qsend, qrecv, key_counts)

    loads[0].wait()
    loads[1].wait()
    asked = spread_heads(qbuf[owned_ref[0]], heads)
    scores = dot_t(asked, pk[...])
    prompt_lane = lax.broadcasted_iota(jnp.int32, scores.shape, 1)
    scores = jnp.where(prompt_lane < plen_ref[0], scores, NEG_FILL)
    top = jnp.max(scores, axis=1, keepdims=True)
    weights = jnp.exp(scores - top).astype(jnp.bfloat16)
    total = jnp.sum(weights.astype(jnp.float32), axis=1, keepdims=True)
    wide = jnp.dot(weights, pv[...], preferred_element_type=jnp.float32) / total
    log_total = top + jnp.log(total)
    stat_lane = lax.broadcasted_iota(jnp.int32, (rows, LANES), 1)
    stats = jnp.zeros((rows, LANES), jnp.float32)
    rest = log_total
    for part in range(3):
        level = rest.astype(jnp.bfloat16).astype(jnp.float32)
        rest = rest - level
        for h in range(heads):
            stats = jnp.where(stat_lane == part * heads + h, level[h * rows : (h + 1) * rows], stats)
    pbuf[me, :, :lanes] = own_columns(wide, rows, lanes).astype(jnp.bfloat16)
    pbuf[me, :, lanes:] = stats.astype(jnp.bfloat16)

    def home_part():
        loads[2].wait()
        loads[3].wait()
        query = spread_heads(q_ref[...], heads)
        pool_c = jnp.concatenate([pool_count] * heads, axis=0)
        new_c = jnp.concatenate([new_count] * heads, axis=0)
        pool_s = jnp.where(pool_c > 0.0, dot_t(query, hk[...]), NEG_FILL)
        new_s = jnp.where(new_c > 0.0, dot_t(query, nk_ref[...]), NEG_FILL)
        home_top = jnp.maximum(
            jnp.max(pool_s, axis=1, keepdims=True), jnp.max(new_s, axis=1, keepdims=True)
        )
        pool_w = jnp.exp(pool_s - home_top).astype(jnp.bfloat16).astype(jnp.float32) * pool_c
        new_w = jnp.exp(new_s - home_top).astype(jnp.bfloat16)
        home_sum = jnp.sum(pool_w, axis=1, keepdims=True) + jnp.sum(
            new_w.astype(jnp.float32), axis=1, keepdims=True
        )
        numer = jnp.dot(pool_w.astype(jnp.bfloat16), hv[...], preferred_element_type=jnp.float32)
        numer = numer + jnp.dot(new_w, nv_ref[...], preferred_element_type=jnp.float32)
        return home_top, home_sum, numer

    (home_top, home_sum, numer), p_sent = gather(pbuf, psend, precv, home_part)

    place = place_ref[0]
    reply = pbuf[place].astype(jnp.float32)
    stats = reply[:, lanes:]
    reply_log = []
    for h in range(heads):
        reply_log.append(
            stats[:, h : h + 1]
            + stats[:, heads + h : heads + h + 1]
            + stats[:, 2 * heads + h : 2 * heads + h + 1]
        )
    reply_log = jnp.concatenate(reply_log, axis=0)
    joint = jnp.maximum(home_top, reply_log)
    home_factor = jnp.exp(home_top - joint)
    prompt_factor = jnp.exp(reply_log - joint)
    scale = 1.0 / (home_sum * home_factor + prompt_factor)
    prompt_wide = jnp.concatenate([reply[:, :lanes]] * heads, axis=0)
    joined = numer * (home_factor * scale) + prompt_wide * (prompt_factor * scale)
    attended = own_columns(joined, rows, lanes).astype(jnp.bfloat16)

    loads[4].wait()
    o_sent = []
    for k in range(OUT_CHUNKS):
        cols = slice(k * chunk, (k + 1) * chunk)
        part = jnp.dot(attended, wo[:, cols], preferred_element_type=jnp.float32)
        obuf[my_tp, k] = part.astype(jnp.bfloat16)
        for peer in tp_peers:
            copy = pltpu.make_async_remote_copy(
                src_ref=obuf.at[my_tp, k], dst_ref=obuf.at[my_tp, k],
                send_sem=osend.at[len(o_sent)], recv_sem=orecv.at[my_tp, k],
                device_id={"tp": peer}, device_id_type=pl.DeviceIdType.MESH,
            )
            copy.start()
            o_sent.append(copy)

    loads[5].wait()
    square = jnp.zeros((rows, 1), jnp.float32)
    for k in range(OUT_CHUNKS):
        cols = slice(k * chunk, (k + 1) * chunk)
        for peer in tp_peers:
            pltpu.make_async_remote_copy(
                src_ref=obuf.at[peer, k], dst_ref=obuf.at[peer, k],
                send_sem=osend.at[0], recv_sem=orecv.at[peer, k],
                device_id={"tp": peer}, device_id_type=pl.DeviceIdType.MESH,
            ).wait_recv()
        summed = obuf[0, k].astype(jnp.float32)
        for t in range(1, tp_size):
            summed = summed + obuf[t, k].astype(jnp.float32)
        mixed = res_ref[:, cols].astype(jnp.float32) + summed
        res_out[:, cols] = mixed.astype(jnp.bfloat16)
        square = square + jnp.sum(mixed * mixed, axis=1, keepdims=True)
        gained = (mixed * gain_ref[:, cols].astype(jnp.float32)).astype(jnp.bfloat16)
        for n in range(3):
            term = jnp.dot(gained, wq[n, cols, :], preferred_element_type=jnp.float32)
            if k == 0:
                acc[n] = term
            else:
                acc[n] += term
    inverse = lax.rsqrt(square / depth + NORM_EPS)
    for n in range(3):
        scaled = acc[n] * inverse
        for s in range(steps):
            qkv_out[s, n] = scaled[s * BEAMS : (s + 1) * BEAMS].astype(jnp.bfloat16)

    for copy in q_sent + p_sent + o_sent:
        copy.wait_send()


def shards(
    queries, new_kv, residual, home_cache, prompt_cache, home_table, home_len,
    parents, prompt_place, owned_request, prompt_len, out_weight, norm_gain, qkv_weight,
):
    steps, beams, lanes = queries.shape
    rows = steps * beams
    depth = residual.shape[2]
    req_size = lax.axis_size("req")
    tp_size = lax.axis_size("tp")
    outer, inner = grid_of(req_size)
    tokens = home_cache.shape[0] * home_cache.shape[1]
    sends = (outer - 1) + outer * (inner - 1) + outer * inner
    smem = pl.BlockSpec(memory_space=pltpu.SMEM)
    vmem = pl.BlockSpec(memory_space=pltpu.VMEM)
    anym = pl.BlockSpec(memory_space=pl.ANY)
    wq = qkv_weight.transpose(1, 0, 2)
    bf16, f32 = jnp.bfloat16, jnp.float32
    dma = pltpu.SemaphoreType.DMA
    qkv, res = pl.pallas_call(
        functools.partial(kernel, req_size, tp_size, steps),
        out_shape=(
            jax.ShapeDtypeStruct((steps, 3, beams, lanes), bf16),
            jax.ShapeDtypeStruct((rows, depth), bf16),
        ),
        in_specs=[smem] * 6 + [vmem] * 5 + [anym] * 6,
        out_specs=(vmem, vmem),
        scratch_shapes=[
            pltpu.VMEM((req_size, rows, lanes), bf16),
            pltpu.VMEM((req_size, rows, lanes + LANES), bf16),
            pltpu.VMEM((tp_size, OUT_CHUNKS, rows, depth // OUT_CHUNKS), bf16),
            pltpu.VMEM((tokens, lanes), bf16),
            pltpu.VMEM((tokens, lanes), bf16),
            pltpu.VMEM((tokens, lanes), bf16),
            pltpu.VMEM((tokens, lanes), bf16),
            pltpu.VMEM(out_weight.shape, bf16),
            pltpu.VMEM(wq.shape, bf16),
            pltpu.VMEM((beams, tokens), f32),
            pltpu.VMEM((3, rows, lanes), f32),
            dma((6,)),
            dma((sends,)),
            dma((req_size,)),
            dma((sends,)),
            dma((req_size,)),
            dma((max(1, OUT_CHUNKS * (tp_size - 1)),)),
            dma((tp_size, OUT_CHUNKS)),
        ],
        compiler_params=pltpu.CompilerParams(
            collective_id=0, has_side_effects=True, vmem_limit_bytes=40 * 1024 * 1024
        ),
    )(
        home_table.T, home_len, parents, prompt_place, owned_request, prompt_len,
        queries.reshape(rows, lanes),
        new_kv[:, :, 0].reshape(rows, lanes),
        new_kv[:, :, 1].reshape(rows, lanes),
        residual.reshape(rows, depth),
        norm_gain.reshape(1, depth),
        home_cache[:, :, 0].reshape(tokens, lanes),
        home_cache[:, :, 1].reshape(tokens, lanes),
        prompt_cache[:, :, 0].reshape(tokens, lanes),
        prompt_cache[:, :, 1].reshape(tokens, lanes),
        out_weight,
        wq,
    )
    return qkv.transpose(0, 2, 1, 3), res.reshape(steps, beams, depth)


def solution(mesh):
    placed = (
        P(None, "req", "tp"),
        P(None, "req", None, "tp"),
        P(None, "req", None),
        P("req", None, None, "tp"),
        P("req", None, None, "tp"),
        P("req", None),
        P("req"),
        P(None, "req"),
        P("req"),
        P("req"),
        P("req"),
        P("tp", None),
        P(),
        P(None, None, "tp"),
    )
    return jax.shard_map(
        shards,
        mesh=mesh,
        in_specs=placed,
        out_specs=(P(None, "req", None, "tp"), P(None, "req", None)),
        check_vma=False,
    )
```

time: 689 us -> 41.2 us (0.06); the launches traced: 679 us -> 41 us
  blocking collectives: 301 us -> 0 us
  local copies, waits for them, and re-layouts: 261 us -> 7.74 us
  matrix products: 63.4 us -> 0 us
  Pallas kernels: 0 us -> 30.5 us
  other arithmetic: 22.4 us -> 0.01 us
  between operations: 17.2 us -> 2.81 us
  waiting for transfers between devices: 13.3 us -> 0 us
    all_gather x16 -> x0, blocking collectives: 301 us -> none  [the longest x4 79.2 us: shards(): all_queries = lax.all_gather(query_block, 'req', axis=1, tiled=True)]
    gather x24 -> x0, local copies, waits for them, and re-layouts: 140 us -> none  [the longest x8 132 us: shards(): home_cache[tables].reshape(row_count, home_tokens, 2, head_count, HEAD_DIM)]
    dot_general x31 -> x0, matrix products: 63.4 us -> none  [the longest x4 18.2 us: shards(): jnp.einsum('bht,bthd->bhd', home_weights, gathered[:, :, 1], preferred_el...]
    reshape x16 -> x1, local copies, waits for them, and re-layouts: 62.4 us -> 0.01 us  [shards(): norm_gain.reshape(1, depth)]
    pallas_call x0 -> x1, Pallas kernels: none -> 30.5 us  [shards(): pl.pallas_call(functools.partial(kernel, req_size, tp_size, steps), out_s...]
    squeeze x7 -> x0, local copies, waits for them, and re-layouts: 24.5 us -> none  [the longest x4 22.5 us: shards(): gathered[:, :, 0]]
    reduce_sum x12 -> x0, other arithmetic: 13.5 us -> none  [the longest x3 5.04 us: shards(): jnp.sum(window_weights.astype(jnp.float32), axis=-1)]
    psum x1 -> x0, waiting for transfers between devices: 13.3 us -> none  [shards(): head_total = lax.psum(projected, 'tp')]
  transfers between devices with their start and end apart: 1 -> 0, of which waited for: 1 -> 0; matrix products, arithmetic and copies ran while one was open for 1% -> 0% of each run, Pallas kernels for 0% -> 0%
where the time goes in v1:
time: 41.2 us; the launch traced here: 41 us
  Pallas kernels  30.5 us (74%)
  local copies, waits for them, and re-layouts  7.74 us (19%)
  between operations  2.81 us (7%)
    pallas_call x1, Pallas kernels, shards(): pl.pallas_call(functools.partial(kernel, req_size, tp_size, steps), out_s...  30.5 us
    slice x1, local copies, waits for them, and re-layouts, shards(): home_cache[:, :, 1].reshape(tokens, lanes)  3.29 us
    unnamed x26, local copies, waits for them, and re-layouts  1.85 us
    slice x1, local copies, waits for them, and re-layouts, shards(): prompt_cache[:, :, 1].reshape(tokens, lanes)  1.5 us
    slice x1, local copies, waits for them, and re-layouts, shards(): new_kv[:, :, 1].reshape(rows, lanes)  1.08 us

profile of v1, /device:TPU:0, one launch (start us, length us, event | category | flops | bytes accessed | tf_op | source)
XLA Modules:
  0.0 41.0 jit_solution(9843265016512257761)
XLA Ops:
  0.6 0.0 copy-start.6
  0.6 1.1 %fusion.2 = (bf16[4,8,1,512]{3,2,1,0:T(2,128)(2,1)S(1)}, bf16[4,8,1,512]{3,2,1,0:T(2,128)(2,1)S(1)}) fusion(bf16[4,8,2,512]{3,2,1,0:T(2,128)(2,1)} %param.15), kind=kLoop, calls=%fused_computation.4 | loop fusion | bytes 131072 | tf_op jit(solution)/shard_map/slice | solution.py:331
  1.7 0.0 slice-start
  1.8 3.3 %fusion.1 = (bf16[4,128,1,512]{3,2,1,0:T(2,128)(2,1)S(1)}, bf16[4,128,1,512]{3,2,1,0:T(2,128)(2,1)S(1)}) fusion(bf16[4,128,2,512]{3,2,1,0:T(2,128)(2,1)} %param.17), kind=kLoop, calls=%fused_computation.3 | loop fusion | bytes 2097152 | tf_op jit(solution)/shard_map/slice | solution.py:335
  5.1 0.0 copy-start.7
  5.1 0.0 copy-start
  5.1 0.0 copy-start.1
  5.1 0.0 copy-start.2
  5.1 0.0 copy-start.3
  5.1 0.0 copy-start.4
  5.1 0.0 copy-start.5
  5.1 0.1 copy.24
  5.3 0.0 slice-start.1
  5.3 0.1 copy.25
  5.4 0.0 copy-done.6
  5.4 1.5 %fusion = (bf16[4,128,1,512]{3,2,1,0:T(2,128)(2,1)S(1)}, bf16[4,128,1,512]{3,2,1,0:T(2,128)(2,1)S(1)}) fusion(bf16[4,128,2,512]{3,2,1,0:T(2,128)(2,1)S(1)} %copy-done.6), kind=kLoop, calls=%fused_computation.2 | loop fusion | bytes 2097152 | tf_op jit(solution)/shard_map/slice | solution.py:337
  6.9 0.1 copy.26
  7.1 0.1 copy.27
  7.2 0.0 copy-done.7
  9.2 0.0 slice-done
  9.2 0.0 copy-done
  9.2 0.0 copy-done.1
  9.2 0.0 copy-done.2
  9.2 0.0 copy-done.3
  9.2 0.0 copy-done.4
  9.2 0.0 copy-done.5
  9.2 0.0 slice-done.1
  9.2 30.5 %shard_map.149 = (bf16[4,3,8,512]{3,2,1,0:T(8,128)(2,1)S(1)}, bf16[32,2048]{1,0:T(8,128)(2,1)S(1)}) custom-call(s32[4,8]{1,0:T(4,128)S(1)} %bitcast.25, s32[8]{0:T(128)S(1)} %copy-done.5, s32[4,8]{1,0:T(4,128)S(1)} %copy-done.4, s32[1]{0:T(128)S(6)} %copy.32.place_ref, s32[1]{0:T(128)S(6)} %copy.33.owned_ref, s32[1]{0:T(128)S(6)} %copy.34.plen_ref, ...), custom_call_target="tpu_custom_call" | custom-call | tf_op jit(solution)/shard_map/pallas_call | solution.py:296
  39.7 0.6 %copy.35 = bf16[4,8,3,512]{3,1,2,0:T(8,128)(2,1)} copy(bf16[4,8,3,512]{3,1,2,0:T(8,128)(2,1)S(1)} %bitcast.23) | data formatting | bytes 196608
  40.4 0.7 %copy.36 = bf16[4,8,2048]{2,1,0:T(8,128)(2,1)} copy(bf16[4,8,2048]{2,1,0:T(8,128)(2,1)S(1)} %bitcast.22) | data formatting | bytes 262144
  (3 shorter events, 0.0 us)
Async XLA Ops:
  0.6 4.8 %copy-start.6 = (bf16[4,128,2,512]{3,2,1,0:T(2,128)(2,1)S(1)}, bf16[4,128,2,512]{3,2,1,0:T(2,128)(2,1)}, u32[]{:S(2)}) copy-start(bf16[4,128,2,512]{3,2,1,0:T(2,128)(2,1)} %param.18) | copy-start | bytes 3145732
  1.7 7.4 %slice-start = ((s8[6291456]{0:T(1024)(128)(4,1)}), s8[4194304]{0:T(1024)(128)(4,1)S(1)}, s32[]{:S(2)}) async-start(s8[6291456]{0:T(1024)(128)(4,1)} %bitcast.14), calls=%async_computation | async-start | bytes 8388608
  5.1 2.1 %copy-start.7 = (bf16[2048]{0:T(1024)(128)(2,1)S(1)}, bf16[2048]{0:T(1024)(128)(2,1)}, u32[]{:S(2)}) copy-start(bf16[2048]{0:T(1024)(128)(2,1)} %param.26) | copy-start | bytes 12292
  5.1 4.1 %copy-start = (bf16[512,2048]{1,0:T(8,128)(2,1)S(1)}, bf16[512,2048]{1,0:T(8,128)(2,1)}, u32[]{:S(2)}) copy-start(bf16[512,2048]{1,0:T(8,128)(2,1)} %wo_hbm.1) | copy-start | bytes 6291460
  5.1 4.1 %copy-start.1 = (bf16[4,8,2048]{2,1,0:T(8,128)(2,1)S(1)}, bf16[4,8,2048]{2,1,0:T(8,128)(2,1)}, u32[]{:S(2)}) copy-start(bf16[4,8,2048]{2,1,0:T(8,128)(2,1)} %param.16) | copy-start | bytes 393220
  5.1 4.1 %copy-start.2 = (bf16[4,8,512]{2,1,0:T(8,128)(2,1)S(1)}, bf16[4,8,512]{2,1,0:T(8,128)(2,1)}, u32[]{:S(2)}) copy-start(bf16[4,8,512]{2,1,0:T(8,128)(2,1)} %param.14) | copy-start | bytes 98308
  5.1 4.1 %copy-start.3 = (s32[8,4]{0,1:T(4,128)S(1)}, s32[8,4]{0,1:T(4,128)}, u32[]{:S(2)}) copy-start(s32[8,4]{0,1:T(4,128)} %param.19) | copy-start | bytes 388
  5.1 4.1 %copy-start.4 = (s32[4,8]{1,0:T(4,128)S(1)}, s32[4,8]{1,0:T(4,128)}, u32[]{:S(2)}) copy-start(s32[4,8]{1,0:T(4,128)} %parents_ref.1) | copy-start | bytes 388
  5.1 4.1 %copy-start.5 = (s32[8]{0:T(128)S(1)}, s32[8]{0:T(128)}, u32[]{:S(2)}) copy-start(s32[8]{0:T(128)} %len_ref.1) | copy-start | bytes 100
  5.3 4.0 %slice-start.1 = ((s8[6291456]{0:T(1024)(128)(4,1)}), s8[2097152]{0:T(1024)(128)(4,1)S(1)}, s32[]{:S(2)}) async-start(s8[6291456]{0:T(1024)(128)(4,1)} %bitcast.14), calls=%async_computation.1 | async-start | bytes 4194304

commit v2 on v1

v2 whole, which is shorter than its diff:
```python
import functools
import math

import jax
import jax.numpy as jnp
from jax import lax
from jax.experimental import pallas as pl
from jax.experimental.pallas import tpu as pltpu
from jax.sharding import PartitionSpec as P

HEAD_DIM = 64
BEAMS = 8
LANES = 128
OUT_CHUNKS = 4
SPLIT = 32

NEG_FILL = -1e30
NORM_EPS = 1e-05


def grid_of(req_size):
    chips = req_size // 2
    outer = 4 if chips % 4 == 0 else 1
    return outer, chips // outer


def spread_heads(q, heads):
    rows, lanes = q.shape
    scaled = q.astype(jnp.float32) * (1.0 / math.sqrt(HEAD_DIM))
    lane_head = lax.broadcasted_iota(jnp.int32, (rows, lanes), 1) // HEAD_DIM
    parts = [jnp.where(lane_head == h, scaled, 0.0) for h in range(heads)]
    return jnp.concatenate(parts, axis=0).astype(jnp.bfloat16)


def dot_t(a, b):
    return lax.dot_general(a, b, (((1,), (1,)), ((), ())), preferred_element_type=jnp.float32)


def own_columns(wide, rows, lanes):
    first = lax.broadcasted_iota(jnp.int32, (rows, LANES), 1) < HEAD_DIM
    tiles = []
    for t in range(lanes // LANES):
        cols = slice(t * LANES, (t + 1) * LANES)
        a = wide[2 * t * rows : (2 * t + 1) * rows, cols]
        b = wide[(2 * t + 1) * rows : (2 * t + 2) * rows, cols]
        tiles.append(jnp.where(first, a, b))
    return tiles[0] if len(tiles) == 1 else jnp.concatenate(tiles, axis=1)


def split_blocks(raw, keys, values):
    tokens, lanes = keys.shape
    kinds = 2 * (lanes // LANES)
    size = SPLIT * kinds
    out_row = lax.broadcasted_iota(jnp.int32, (size, size), 0)
    in_row = lax.broadcasted_iota(jnp.int32, (size, size), 1)
    wanted = (out_row % SPLIT) * kinds + out_row // SPLIT
    order = jnp.where(in_row == wanted, 1.0, 0.0).astype(jnp.bfloat16)
    for n in range(tokens // SPLIT):
        sorted_rows = jnp.dot(
            order, raw[n * size : (n + 1) * size, :], preferred_element_type=jnp.float32
        ).astype(jnp.bfloat16)
        for t in range(lanes // LANES):
            at = 2 * t * SPLIT
            rows, cols = slice(n * SPLIT, (n + 1) * SPLIT), slice(t * LANES, (t + 1) * LANES)
            keys[rows, cols] = sorted_rows[at : at + SPLIT]
            values[rows, cols] = sorted_rows[at + SPLIT : at + 2 * SPLIT]


def kernel(
    req_size, tp_size, steps,
    table_any, len_any, parents_any, place_any, owned_any, plen_any,
    q_any, new_any, res_any, gain_any, home_any, prompt_any, wo_any, wq_any,
    qkv_out, res_out,
    table_ref, len_ref, parents_ref, place_ref, owned_ref, plen_ref,
    q_ref, new_raw, res_ref, gain_ref, home_raw, prompt_raw, wo, wq,
    meta, qz, qmsg, qplane, rz, rmsg, rplane, obuf,
    nk, nv, hk, hv, pk, pv, base, acc,
    load_sem, msend, mrecv, qzsend, qzrecv, qpsend, qprecv,
    rzsend, rzrecv, rpsend, rprecv, osend, orecv,
):
    rows, lanes = q_ref.shape
    heads = lanes // HEAD_DIM
    depth = res_ref.shape[1]
    chunk = depth // OUT_CHUNKS
    tokens = hk.shape[0]
    block_count = table_ref.shape[0]
    block = tokens // block_count
    outer, inner = grid_of(req_size)
    planes = 2 * inner
    me = lax.axis_index("req")
    my_tp = lax.axis_index("tp")
    o = me // planes
    p = lax.rem(me, planes)

    mesh_id = pl.DeviceIdType.MESH
    outer_peers = [lax.rem(o + d, outer) * planes + p for d in range(1, outer)]
    plane_peers = [lax.rem(p + d, planes) for d in range(1, planes)]
    tp_peers = [lax.rem(my_tp + d, tp_size) for d in range(1, tp_size)]

    barrier = pltpu.get_barrier_semaphore()
    for peer in outer_peers + [o * planes + pp for pp in plane_peers]:
        pl.semaphore_signal(barrier, inc=1, device_id={"req": peer}, device_id_type=mesh_id)
    for peer in tp_peers:
        pl.semaphore_signal(barrier, inc=1, device_id={"tp": peer}, device_id_type=mesh_id)

    pairs = [
        (q_any, q_ref), (place_any, place_ref), (owned_any, owned_ref), (plen_any, plen_ref),
        (table_any, table_ref), (len_any, len_ref), (parents_any, parents_ref),
        (prompt_any, prompt_raw), (home_any, home_raw), (new_any, new_raw),
        (wo_any, wo), (res_any, res_ref), (gain_any, gain_ref), (wq_any, wq),
    ]
    loads = [pltpu.make_async_copy(src, dst, load_sem.at[n]) for n, (src, dst) in enumerate(pairs)]
    for copy in loads:
        copy.start()
    sent = []

    def push(src, dst, send_sem, recv_sem, axis, peer):
        copy = pltpu.make_async_remote_copy(
            src_ref=src, dst_ref=dst, send_sem=send_sem, recv_sem=recv_sem,
            device_id={axis: peer}, device_id_type=mesh_id,
        )
        copy.start()
        sent.append(copy)

    def arrive(dst, send_sem, recv_sem, axis, peer):
        pltpu.make_async_remote_copy(
            src_ref=dst, dst_ref=dst, send_sem=send_sem, recv_sem=recv_sem,
            device_id={axis: peer}, device_id_type=mesh_id,
        ).wait_recv()

    def send_outer(buf, send, recv):
        for d in reversed(range(1, outer)):
            push(buf.at[o], buf.at[o], send.at[d - 1], recv.at[o], "req", outer_peers[d - 1])

    def wait_outer(buf, send, recv):
        for d in range(1, outer):
            slot = lax.rem(o + d, outer)
            arrive(buf.at[slot], send.at[0], recv.at[slot], "req", outer_peers[d - 1])

    def send_plane(buf, marks, msg, landed, send, recv):
        held = [buf[s].astype(jnp.float32) for s in range(outer)]

        def chosen(target):
            value = held[0]
            for s in range(1, outer):
                value = jnp.where(marks[s] == target.astype(jnp.float32), held[s], value)
            return value.astype(jnp.bfloat16)

        for d, pp in enumerate(plane_peers):
            msg[d] = chosen(o * planes + pp)
            push(msg.at[d], landed.at[p], send.at[d], recv.at[p], "req", o * planes + pp)
        landed[p] = chosen(me)

    def wait_plane(landed, send, recv):
        for pp in plane_peers:
            arrive(landed.at[pp], send.at[0], recv.at[pp], "req", o * planes + pp)

    def key_counts():
        lane = lax.broadcasted_iota(jnp.int32, (1, tokens), 1)
        lane_block = lane // block
        lane_pos = lane - lane_block * block
        for b in range(BEAMS):
            total = jnp.zeros((1, tokens), jnp.float32)
            for j in range(block_count):
                live = (lane_block == table_ref[j, b]) & (lane_pos + j * block < len_ref[b])
                total = total + jnp.where(live, 1.0, 0.0)
            base[b : b + 1, :] = total
        pool = base[...]
        row8 = lax.broadcasted_iota(jnp.int32, (BEAMS, BEAMS), 0)
        col8 = lax.broadcasted_iota(jnp.int32, (BEAMS, BEAMS), 1)
        new_row = lax.broadcasted_iota(jnp.int32, (BEAMS, rows), 0)
        new_col = lax.broadcasted_iota(jnp.int32, (BEAMS, rows), 1)
        new = jnp.zeros((BEAMS, rows), jnp.float32)
        pools, news = [], []
        for s in range(steps):
            pick = jnp.zeros((BEAMS, BEAMS), jnp.float32)
            for b in range(BEAMS):
                pick = jnp.where((row8 == b) & (col8 == parents_ref[s, b]), 1.0, pick)
            pool = jnp.dot(pick, pool, preferred_element_type=jnp.float32)
            new = jnp.dot(pick, new, preferred_element_type=jnp.float32)
            new = new + jnp.where(new_col == new_row + s * BEAMS, 1.0, 0.0)
            pools.append(pool)
            news.append(new)
        return jnp.concatenate(pools, axis=0), jnp.concatenate(news, axis=0)

    for copy in loads[:7]:
        copy.wait()
    meta_lane = lax.broadcasted_iota(jnp.int32, (16, LANES), 1)
    meta[o] = (
        jnp.where(meta_lane < LANES // 2, place_ref[0], owned_ref[0])
        .astype(jnp.float32)
        .astype(jnp.bfloat16)
    )
    qz[o] = q_ref[...]
    pl.semaphore_wait(barrier, len(outer_peers) + len(plane_peers) + len(tp_peers))
    send_outer(meta, msend, mrecv)
    send_outer(qz, qzsend, qzrecv)
    pool_count, new_count = key_counts()
    loads[7].wait()
    split_blocks(prompt_raw, pk, pv)
    wait_outer(meta, msend, mrecv)
    marks = [meta[s].astype(jnp.float32) for s in range(outer)]
    place_marks = [mark[0:1, 0:1] for mark in marks]
    owned_marks = [mark[0:1, LANES // 2 : LANES // 2 + 1] for mark in marks]
    wait_outer(qz, qzsend, qzrecv)
    send_plane(qz, place_marks, qmsg, qplane, qpsend, qprecv)
    loads[8].wait()
    loads[9].wait()
    split_blocks(home_raw, hk, hv)
    split_blocks(new_raw, nk, nv)
    wait_plane(qplane, qpsend, qprecv)

    asked = spread_heads(qplane[lax.rem(owned_ref[0], planes)], heads)
    scores = dot_t(asked, pk[...])
    prompt_lane = lax.broadcasted_iota(jnp.int32, scores.shape, 1)
    scores = jnp.where(prompt_lane < plen_ref[0], scores, NEG_FILL)
    top = jnp.max(scores, axis=1, keepdims=True)
    weights = jnp.exp(scores - top).astype(jnp.bfloat16)
    total = jnp.sum(weights.astype(jnp.float32), axis=1, keepdims=True)
    wide = jnp.dot(weights, pv[...], preferred_element_type=jnp.float32) / total
    log_total = top + jnp.log(total)
    stat_lane = lax.broadcasted_iota(jnp.int32, (rows, LANES), 1)
    stats = jnp.zeros((rows, LANES), jnp.float32)
    rest = log_total
    for part in range(3):
        level = rest.astype(jnp.bfloat16).astype(jnp.float32)
        rest = rest - level
        for h in range(heads):
            stats = jnp.where(stat_lane == part * heads + h, level[h * rows : (h + 1) * rows], stats)
    rz[o, :, :lanes] = own_columns(wide, rows, lanes).astype(jnp.bfloat16)
    rz[o, :, lanes:] = stats.astype(jnp.bfloat16)
    send_outer(rz, rzsend, rzrecv)

    query = spread_heads(q_ref[...], heads)
    pool_c = jnp.concatenate([pool_count] * heads, axis=0)
    new_c = jnp.concatenate([new_count] * heads, axis=0)
    pool_s = jnp.where(pool_c > 0.0, dot_t(query, hk[...]), NEG_FILL)
    new_s = jnp.where(new_c > 0.0, dot_t(query, nk[...]), NEG_FILL)
    home_top = jnp.maximum(
        jnp.max(pool_s, axis=1, keepdims=True), jnp.max(new_s, axis=1, keepdims=True)
    )
    pool_w = jnp.exp(pool_s - home_top).astype(jnp.bfloat16).astype(jnp.float32) * pool_c
    new_w = jnp.exp(new_s - home_top).astype(jnp.bfloat16)
    home_sum = jnp.sum(pool_w, axis=1, keepdims=True) + jnp.sum(
        new_w.astype(jnp.float32), axis=1, keepdims=True
    )
    numer = jnp.dot(pool_w.astype(jnp.bfloat16), hv[...], preferred_element_type=jnp.float32)
    numer = numer + jnp.dot(new_w, nv[...], preferred_element_type=jnp.float32)

    wait_outer(rz, rzsend, rzrecv)
    send_plane(rz, owned_marks, rmsg, rplane, rpsend, rprecv)
    wait_plane(rplane, rpsend, rprecv)
    reply = rplane[lax.rem(place_ref[0], planes)].astype(jnp.float32)
    stats = reply[:, lanes:]
    reply_log = []
    for h in range(heads):
        reply_log.append(
            stats[:, h : h + 1]
            + stats[:, heads + h : heads + h + 1]
            + stats[:, 2 * heads + h : 2 * heads + h + 1]
        )
    reply_log = jnp.concatenate(reply_log, axis=0)
    joint = jnp.maximum(home_top, reply_log)
    home_factor = jnp.exp(home_top - joint)
    prompt_factor = jnp.exp(reply_log - joint)
    scale = 1.0 / (home_sum * home_factor + prompt_factor)
    prompt_wide = jnp.concatenate([reply[:, :lanes]] * heads, axis=0)
    joined = numer * (home_factor * scale) + prompt_wide * (prompt_factor * scale)
    attended = own_columns(joined, rows, lanes).astype(jnp.bfloat16)

    loads[10].wait()
    for k in range(OUT_CHUNKS):
        cols = slice(k * chunk, (k + 1) * chunk)
        part = jnp.dot(attended, wo[:, cols], preferred_element_type=jnp.float32)
        obuf[my_tp, k] = part.astype(jnp.bfloat16)
        for d, peer in enumerate(tp_peers):
            mine = obuf.at[my_tp, k]
            push(mine, mine, osend.at[k * len(tp_peers) + d], orecv.at[my_tp, k], "tp", peer)

    for copy in loads[11:]:
        copy.wait()
    square = jnp.zeros((rows, 1), jnp.float32)
    for k in range(OUT_CHUNKS):
        cols = slice(k * chunk, (k + 1) * chunk)
        for peer in tp_peers:
            arrive(obuf.at[peer, k], osend.at[0], orecv.at[peer, k], "tp", peer)
        summed = obuf[0, k].astype(jnp.float32)
        for t in range(1, tp_size):
            summed = summed + obuf[t, k].astype(jnp.float32)
        mixed = res_ref[:, cols].astype(jnp.float32) + summed
        res_out[:, cols] = mixed.astype(jnp.bfloat16)
        square = square + jnp.sum(mixed * mixed, axis=1, keepdims=True)
        gained = (mixed * gain_ref[:, cols].astype(jnp.float32)).astype(jnp.bfloat16)
        for n in range(3):
            term = jnp.dot(gained, wq[n, cols, :], preferred_element_type=jnp.float32)
            if k == 0:
                acc[n] = term
            else:
                acc[n] += term
    inverse = lax.rsqrt(square / depth + NORM_EPS)
    for n in range(3):
        scaled = acc[n] * inverse
        for s in range(steps):
            qkv_out[s, n] = scaled[s * BEAMS : (s + 1) * BEAMS].astype(jnp.bfloat16)

    for copy in sent:
        copy.wait_send()


def token_rows(cache):
    lanes = cache.shape[-1]
    tiles = cache.reshape(-1, 2, lanes // LANES, LANES).transpose(0, 2, 1, 3)
    return tiles.reshape(-1, LANES)


def shards(
    queries, new_kv, residual, home_cache, prompt_cache, home_table, home_len,
    parents, prompt_place, owned_request, prompt_len, out_weight, norm_gain, qkv_weight,
):
    steps, beams, lanes = queries.shape
    rows = steps * beams
    depth = residual.shape[2]
    req_size = lax.axis_size("req")
    tp_size = lax.axis_size("tp")
    outer, inner = grid_of(req_size)
    planes = 2 * inner
    tokens = home_cache.shape[0] * home_cache.shape[1]
    vmem = pl.BlockSpec(memory_space=pltpu.VMEM)
    hbm = pl.BlockSpec(memory_space=pltpu.HBM)
    bf16, f32 = jnp.bfloat16, jnp.float32
    dma = pltpu.SemaphoreType.DMA
    ints = (home_table.T, home_len, parents, prompt_place, owned_request, prompt_len)
    floats = (
        queries.reshape(rows, lanes),
        token_rows(new_kv),
        residual.reshape(rows, depth),
        norm_gain.reshape(1, depth),
        token_rows(home_cache),
        token_rows(prompt_cache),
        out_weight,
        qkv_weight.transpose(1, 0, 2),
    )
    wide = lanes + LANES
    sems = [
        (len(ints) + len(floats),),
        (outer,), (outer,), (outer,), (outer,), (planes,), (planes,),
        (outer,), (outer,), (planes,), (planes,),
        (OUT_CHUNKS * tp_size,), (tp_size, OUT_CHUNKS),
    ]
    qkv, res = pl.pallas_call(
        functools.partial(kernel, req_size, tp_size, steps),
        out_shape=(
            jax.ShapeDtypeStruct((steps, 3, beams, lanes), bf16),
            jax.ShapeDtypeStruct((rows, depth), bf16),
        ),
        in_specs=[hbm] * (len(ints) + len(floats)),
        out_specs=(vmem, vmem),
        scratch_shapes=[pltpu.SMEM(a.shape, jnp.int32) for a in ints]
        + [pltpu.VMEM(a.shape, bf16) for a in floats]
        + [
            pltpu.VMEM((outer, 16, LANES), bf16),
            pltpu.VMEM((outer, rows, lanes), bf16),
            pltpu.VMEM((planes - 1, rows, lanes), bf16),
            pltpu.VMEM((planes, rows, lanes), bf16),
            pltpu.VMEM((outer, rows, wide), bf16),
            pltpu.VMEM((planes - 1, rows, wide), bf16),
            pltpu.VMEM((planes, rows, wide), bf16),
            pltpu.VMEM((tp_size, OUT_CHUNKS, rows, depth // OUT_CHUNKS), bf16),
            pltpu.VMEM((rows, lanes), bf16),
            pltpu.VMEM((rows, lanes), bf16),
            pltpu.VMEM((tokens, lanes), bf16),
            pltpu.VMEM((tokens, lanes), bf16),
            pltpu.VMEM((tokens, lanes), bf16),
            pltpu.VMEM((tokens, lanes), bf16),
            pltpu.VMEM((beams, tokens), f32),
            pltpu.VMEM((3, rows, lanes), f32),
        ]
        + [dma(shape) for shape in sems],
        compiler_params=pltpu.CompilerParams(
            collective_id=0, has_side_effects=True, vmem_limit_bytes=56 * 1024 * 1024
        ),
    )(*ints, *floats)
    return qkv.transpose(0, 2, 1, 3), res.reshape(steps, beams, depth)


def solution(mesh):
    placed = (
        P(None, "req", "tp"),
        P(None, "req", None, "tp"),
        P(None, "req", None),
        P("req", None, None, "tp"),
        P("req", None, None, "tp"),
        P("req", None),
        P("req"),
        P(None, "req"),
        P("req"),
        P("req"),
        P("req"),
        P("tp", None),
        P(),
        P(None, None, "tp"),
    )
    return jax.shard_map(
        shards,
        mesh=mesh,
        in_specs=placed,
        out_specs=(P(None, "req", None, "tp"), P(None, "req", None)),
        check_vma=False,
    )
```

time: 41.2 us -> 37 us (0.90)
  local copies, waits for them, and re-layouts: 7.74 us -> 4.4 us
  Pallas kernels: 30.5 us -> 29.8 us
    slice x3 -> x0, local copies, waits for them, and re-layouts: 5.87 us -> none  [the longest x1 3.29 us: shards(): home_cache[:, :, 1].reshape(tokens, lanes)]
    reshape x1, local copies, waits for them, and re-layouts: 0.01 us -> 1.29 us  [shards(): norm_gain.reshape(1, depth)]
    unnamed x26 -> x2, local copies, waits for them, and re-layouts: 1.85 us -> 3.11 us
    pallas_call x1, Pallas kernels: 30.5 us -> 29.8 us  [shards(): pl.pallas_call(functools.partial(kernel, req_size, tp_size, steps), out_s...]
where the time goes in v2:
time: 37 us; the launch traced here: 36.7 us
  Pallas kernels  29.8 us (81%)
  local copies, waits for them, and re-layouts  4.4 us (12%)
  between operations  2.58 us (7%)
    pallas_call x1, Pallas kernels, shards(): pl.pallas_call(functools.partial(kernel, req_size, tp_size, steps), out_s...  29.8 us
    unnamed x2, local copies, waits for them, and re-layouts  3.11 us
    reshape x1, local copies, waits for them, and re-layouts, shards(): norm_gain.reshape(1, depth)  1.29 us

profile of v2, /device:TPU:0, one launch (start us, length us, event | category | flops | bytes accessed | tf_op | source)
XLA Modules:
  0.0 36.7 jit_solution(14089895207034454374)
XLA Ops:
  2.6 1.3 %reshape.38.gain_any = bf16[1,2048]{1,0:T(2,128)(2,1)} reshape(bf16[2048]{0:T(1024)(128)(2,1)} %param.26) | data formatting | bytes 8192 | tf_op jit(solution)/shard_map/reshape | solution.py:337
  3.9 29.8 %shard_map.149 = (bf16[4,3,8,512]{3,2,1,0:T(8,128)(2,1)}, bf16[32,2048]{1,0:T(8,128)(2,1)}) custom-call(s32[4,8]{1,0:T(4,128)} %bitcast.29, s32[8]{0:T(128)} %len_any.1, s32[4,8]{1,0:T(4,128)} %parents_any.1, s32[1]{0:T(128)S(6)} %copy.21.place_any, s32[1]{0:T(128)S(6)} %copy.22.owned_any, s32[1]{0:T(128)S(6)} %copy.23.plen_any, bf16[32,512]{1,0:T(8,128)(2,1)} %bitcast.28, ...), custom_call_target="tpu_custom_call" | custom-call | tf_op jit(solution)/shard_map/pallas_call | solution.py:350
  33.6 1.5 %copy.24 = bf16[4,8,3,512]{3,1,2,0:T(8,128)(2,1)} copy(bf16[4,8,3,512]{3,1,2,0:T(8,128)(2,1)} %bitcast.26) | data formatting | bytes 196608
  35.2 1.6 %copy.25 = bf16[4,8,2048]{2,1,0:T(8,128)(2,1)} copy(bf16[4,8,2048]{2,1,0:T(8,128)(2,1)} %bitcast.25) | data formatting | bytes 262144

commit v3 on v2

--- a/solution.py
+++ b/solution.py
@@ -36,14 +36,12 @@
     return lax.dot_general(a, b, (((1,), (1,)), ((), ())), preferred_element_type=jnp.float32)
 
 
-def own_columns(wide, rows, lanes):
+def own_columns(rows, lanes, piece):
     first = lax.broadcasted_iota(jnp.int32, (rows, LANES), 1) < HEAD_DIM
     tiles = []
     for t in range(lanes // LANES):
         cols = slice(t * LANES, (t + 1) * LANES)
-        a = wide[2 * t * rows : (2 * t + 1) * rows, cols]
-        b = wide[(2 * t + 1) * rows : (2 * t + 2) * rows, cols]
-        tiles.append(jnp.where(first, a, b))
+        tiles.append(jnp.where(first, piece(2 * t, cols), piece(2 * t + 1, cols)))
     return tiles[0] if len(tiles) == 1 else jnp.concatenate(tiles, axis=1)
 
 
@@ -68,15 +66,14 @@
 
 def kernel(
     req_size, tp_size, steps,
-    table_any, len_any, parents_any, place_any, owned_any, plen_any,
+    place_ref, owned_ref, plen_ref, table_any, len_any, parents_any,
     q_any, new_any, res_any, gain_any, home_any, prompt_any, wo_any, wq_any,
     qkv_out, res_out,
-    table_ref, len_ref, parents_ref, place_ref, owned_ref, plen_ref,
+    table_ref, len_ref, parents_ref,
     q_ref, new_raw, res_ref, gain_ref, home_raw, prompt_raw, wo, wq,
-    meta, qz, qmsg, qplane, rz, rmsg, rplane, obuf,
+    meta_c, meta_p, qa, qa_msg, qa_in, qb, qb_msg, qb_in, ra, ra_msg, ra_in, rb, rb_msg, rb_in, obuf,
     nk, nv, hk, hv, pk, pv, base, acc,
-    load_sem, msend, mrecv, qzsend, qzrecv, qpsend, qprecv,
-    rzsend, rzrecv, rpsend, rprecv, osend, orecv,
+    load_sem, osend, orecv, *hop_sems
 ):
     rows, lanes = q_ref.shape
     heads = lanes // HEAD_DIM
@@ -92,20 +89,28 @@
     o = me // planes
     p = lax.rem(me, planes)
 
+    half = rows // 2
     mesh_id = pl.DeviceIdType.MESH
-    outer_peers = [lax.rem(o + d, outer) * planes + p for d in range(1, outer)]
-    plane_peers = [lax.rem(p + d, planes) for d in range(1, planes)]
+    column = (outer, o, lambda n: n * planes + p)
+    plane = (planes, p, lambda n: o * planes + n)
+
+    def others(group):
+        size, mine, _ = group
+        return [lax.rem(mine + d, size) for d in range(1, size)]
+
+    sem_pairs = [hop_sems[n : n + 2] for n in range(0, len(hop_sems), 2)]
+    meta_c_sem, meta_p_sem, qa_sem, qa2_sem, qb_sem, qb2_sem, ra_sem, ra2_sem, rb_sem, rb2_sem = sem_pairs
     tp_peers = [lax.rem(my_tp + d, tp_size) for d in range(1, tp_size)]
 
     barrier = pltpu.get_barrier_semaphore()
-    for peer in outer_peers + [o * planes + pp for pp in plane_peers]:
-        pl.semaphore_signal(barrier, inc=1, device_id={"req": peer}, device_id_type=mesh_id)
+    for group in (column, plane):
+        for n in others(group):
+            pl.semaphore_signal(barrier, inc=1, device_id={"req": group[2](n)}, device_id_type=mesh_id)
     for peer in tp_peers:
         pl.semaphore_signal(barrier, inc=1, device_id={"tp": peer}, device_id_type=mesh_id)
 
     pairs = [
-        (q_any, q_ref), (place_any, place_ref), (owned_any, owned_ref), (plen_any, plen_ref),
-        (table_any, table_ref), (len_any, len_ref), (parents_any, parents_ref),
+        (q_any, q_ref), (table_any, table_ref), (len_any, len_ref), (parents_any, parents_ref),
         (prompt_any, prompt_raw), (home_any, home_raw), (new_any, new_raw),
         (wo_any, wo), (res_any, res_ref), (gain_any, gain_ref), (wq_any, wq),
     ]
@@ -128,32 +133,29 @@
             device_id={axis: peer}, device_id_type=mesh_id,
         ).wait_recv()
 
-    def send_outer(buf, send, recv):
-        for d in reversed(range(1, outer)):
-            push(buf.at[o], buf.at[o], send.at[d - 1], recv.at[o], "req", outer_peers[d - 1])
-
-    def wait_outer(buf, send, recv):
-        for d in range(1, outer):
-            slot = lax.rem(o + d, outer)
-            arrive(buf.at[slot], send.at[0], recv.at[slot], "req", outer_peers[d - 1])
-
-    def send_plane(buf, marks, msg, landed, send, recv):
-        held = [buf[s].astype(jnp.float32) for s in range(outer)]
+    def first_hop(buf, group, sems):
+        _, mine, index = group
+        for d, n in enumerate(others(group)):
+            push(buf.at[mine], buf.at[mine], sems[0].at[d], sems[1].at[mine], "req", index(n))
+
+    def wait_hop(buf, group, sems):
+        for n in others(group):
+            arrive(buf.at[n], sems[0].at[0], sems[1].at[n], "req", group[2](n))
+
+    def second_hop(buf, marks, msg, landed, group, sems):
+        held = [buf[s].astype(jnp.float32) for s in range(buf.shape[0])]
+        _, mine, index = group
 
         def chosen(target):
             value = held[0]
-            for s in range(1, outer):
+            for s in range(1, len(held)):
                 value = jnp.where(marks[s] == target.astype(jnp.float32), held[s], value)
             return value.astype(jnp.bfloat16)
 
-        for d, pp in enumerate(plane_peers):
-            msg[d] = chosen(o * planes + pp)
-            push(msg.at[d], landed.at[p], send.at[d], recv.at[p], "req", o * planes + pp)
-        landed[p] = chosen(me)
-
-    def wait_plane(landed, send, recv):
-        for pp in plane_peers:
-            arrive(landed.at[pp], send.at[0], recv.at[pp], "req", o * planes + pp)
+        for d, n in enumerate(others(group)):
+            msg[d] = chosen(index(n))
+            push(msg.at[d], landed.at[mine], sems[0].at[d], sems[1].at[mine], "req", index(n))
+        landed[mine] = chosen(me)
 
     def key_counts():
         lane = lax.broadcasted_iota(jnp.int32, (1, tokens), 1)
@@ -183,41 +185,58 @@
             news.append(new)
         return jnp.concatenate(pools, axis=0), jnp.concatenate(news, axis=0)
 
-    for copy in loads[:7]:
+    for copy in loads[:4]:
         copy.wait()
     meta_lane = lax.broadcasted_iota(jnp.int32, (16, LANES), 1)
-    meta[o] = (
+    mark = (
         jnp.where(meta_lane < LANES // 2, place_ref[0], owned_ref[0])
         .astype(jnp.float32)
         .astype(jnp.bfloat16)
     )
-    qz[o] = q_ref[...]
-    pl.semaphore_wait(barrier, len(outer_peers) + len(plane_peers) + len(tp_peers))
-    send_outer(meta, msend, mrecv)
-    send_outer(qz, qzsend, qzrecv)
+    meta_c[o] = mark
+    meta_p[p] = mark
+    qa[o] = q_ref[:half, :]
+    qb[p] = q_ref[half:, :]
+    pl.semaphore_wait(barrier, outer - 1 + planes - 1 + len(tp_peers))
+    first_hop(meta_p, plane, meta_p_sem)
+    first_hop(qb, plane, qb_sem)
+    first_hop(meta_c, column, meta_c_sem)
+    first_hop(qa, column, qa_sem)
     pool_count, new_count = key_counts()
-    loads[7].wait()
+
+    def marks_of(meta):
+        rows_of = [meta[s].astype(jnp.float32) for s in range(meta.shape[0])]
+        middle = LANES // 2
+        return [r[0:1, 0:1] for r in rows_of], [r[0:1, middle : middle + 1] for r in rows_of]
+
+    wait_hop(meta_p, plane, meta_p_sem)
+    places_p, owners_p = marks_of(meta_p)
+    wait_hop(qb, plane, qb_sem)
+    second_hop(qb, places_p, qb_msg, qb_in, column, qb2_sem)
+    loads[4].wait()
     split_blocks(prompt_raw, pk, pv)
-    wait_outer(meta, msend, mrecv)
-    marks = [meta[s].astype(jnp.float32) for s in range(outer)]
-    place_marks = [mark[0:1, 0:1] for mark in marks]
-    owned_marks = [mark[0:1, LANES // 2 : LANES // 2 + 1] for mark in marks]
-    wait_outer(qz, qzsend, qzrecv)
-    send_plane(qz, place_marks, qmsg, qplane, qpsend, qprecv)
-    loads[8].wait()
-    loads[9].wait()
+    wait_hop(meta_c, column, meta_c_sem)
+    places_c, owners_c = marks_of(meta_c)
+    wait_hop(qa, column, qa_sem)
+    second_hop(qa, places_c, qa_msg, qa_in, plane, qa2_sem)
+    loads[5].wait()
+    loads[6].wait()
     split_blocks(home_raw, hk, hv)
     split_blocks(new_raw, nk, nv)
-    wait_plane(qplane, qpsend, qprecv)
-
-    asked = spread_heads(qplane[lax.rem(owned_ref[0], planes)], heads)
+    wait_hop(qa_in, plane, qa2_sem)
+    wait_hop(qb_in, column, qb2_sem)
+
+    owned = owned_ref[0]
+    asked = jnp.concatenate([qa_in[lax.rem(owned, planes)], qb_in[owned // planes]], axis=0)
+    asked = spread_heads(asked, heads)
     scores = dot_t(asked, pk[...])
     prompt_lane = lax.broadcasted_iota(jnp.int32, scores.shape, 1)
     scores = jnp.where(prompt_lane < plen_ref[0], scores, NEG_FILL)
     top = jnp.max(scores, axis=1, keepdims=True)
     weights = jnp.exp(scores - top).astype(jnp.bfloat16)
     total = jnp.sum(weights.astype(jnp.float32), axis=1, keepdims=True)
-    wide = jnp.dot(weights, pv[...], preferred_element_type=jnp.float32) / total
+    wide = jnp.dot(weights, pv[...], preferred_element_type=jnp.float32)
+    part_of = 1.0 / total
     log_total = top + jnp.log(total)
     stat_lane = lax.broadcasted_iota(jnp.int32, (rows, LANES), 1)
     stats = jnp.zeros((rows, LANES), jnp.float32)
@@ -227,10 +246,21 @@
         rest = rest - level
         for h in range(heads):
             stats = jnp.where(stat_lane == part * heads + h, level[h * rows : (h + 1) * rows], stats)
-    rz[o, :, :lanes] = own_columns(wide, rows, lanes).astype(jnp.bfloat16)
-    rz[o, :, lanes:] = stats.astype(jnp.bfloat16)
-    send_outer(rz, rzsend, rzrecv)
-
+    def answer(h, cols):
+        own = slice(h * rows, (h + 1) * rows)
+        return wide[own, cols] * part_of[own]
+
+    answers = own_columns(rows, lanes, answer).astype(jnp.bfloat16)
+    stats = stats.astype(jnp.bfloat16)
+    rb[p, :, :lanes] = answers[half:]
+    rb[p, :, lanes:] = stats[half:]
+    ra[o, :, :lanes] = answers[:half]
+    ra[o, :, lanes:] = stats[:half]
+    first_hop(rb, plane, rb_sem)
+    first_hop(ra, column, ra_sem)
+
+    wait_hop(rb, plane, rb_sem)
+    second_hop(rb, owners_p, rb_msg, rb_in, column, rb2_sem)
     query = spread_heads(q_ref[...], heads)
     pool_c = jnp.concatenate([pool_count] * heads, axis=0)
     new_c = jnp.concatenate([new_count] * heads, axis=0)
@@ -247,10 +277,13 @@
     numer = jnp.dot(pool_w.astype(jnp.bfloat16), hv[...], preferred_element_type=jnp.float32)
     numer = numer + jnp.dot(new_w, nv[...], preferred_element_type=jnp.float32)
 
-    wait_outer(rz, rzsend, rzrecv)
-    send_plane(rz, owned_marks, rmsg, rplane, rpsend, rprecv)
-    wait_plane(rplane, rpsend, rprecv)
-    reply = rplane[lax.rem(place_ref[0], planes)].astype(jnp.float32)
+    wait_hop(ra, column, ra_sem)
+    second_hop(ra, owners_c, ra_msg, ra_in, plane, ra2_sem)
+    wait_hop(ra_in, plane, ra2_sem)
+    wait_hop(rb_in, column, rb2_sem)
+    place = place_ref[0]
+    reply = jnp.concatenate([ra_in[lax.rem(place, planes)], rb_in[place // planes]], axis=0)
+    reply = reply.astype(jnp.float32)
     stats = reply[:, lanes:]
     reply_log = []
     for h in range(heads):
@@ -264,11 +297,16 @@
     home_factor = jnp.exp(home_top - joint)
     prompt_factor = jnp.exp(reply_log - joint)
     scale = 1.0 / (home_sum * home_factor + prompt_factor)
-    prompt_wide = jnp.concatenate([reply[:, :lanes]] * heads, axis=0)
-    joined = numer * (home_factor * scale) + prompt_wide * (prompt_factor * scale)
-    attended = own_columns(joined, rows, lanes).astype(jnp.bfloat16)
-
-    loads[10].wait()
+    home_factor = home_factor * scale
+    prompt_factor = prompt_factor * scale
+
+    def joined(h, cols):
+        own = slice(h * rows, (h + 1) * rows)
+        return numer[own, cols] * home_factor[own] + reply[:, cols] * prompt_factor[own]
+
+    attended = own_columns(rows, lanes, joined).astype(jnp.bfloat16)
+
+    loads[7].wait()
     for k in range(OUT_CHUNKS):
         cols = slice(k * chunk, (k + 1) * chunk)
         part = jnp.dot(attended, wo[:, cols], preferred_element_type=jnp.float32)
@@ -277,8 +315,9 @@
             mine = obuf.at[my_tp, k]
             push(mine, mine, osend.at[k * len(tp_peers) + d], orecv.at[my_tp, k], "tp", peer)
 
-    for copy in loads[11:]:
+    for copy in loads[8:]:
         copy.wait()
+    gain_all = gain_ref[...].astype(jnp.float32)
     square = jnp.zeros((rows, 1), jnp.float32)
     for k in range(OUT_CHUNKS):
         cols = slice(k * chunk, (k + 1) * chunk)
@@ -290,7 +329,8 @@
         mixed = res_ref[:, cols].astype(jnp.float32) + summed
         res_out[:, cols] = mixed.astype(jnp.bfloat16)
         square = square + jnp.sum(mixed * mixed, axis=1, keepdims=True)
-        gained = (mixed * gain_ref[:, cols].astype(jnp.float32)).astype(jnp.bfloat16)
+        gain_rows = [gain_all[n : n + 1] for n in range(k * chunk // LANES, (k + 1) * chunk // LANES)]
+        gained = (mixed * jnp.concatenate(gain_rows, axis=1)).astype(jnp.bfloat16)
         for n in range(3):
             term = jnp.dot(gained, wq[n, cols, :], preferred_element_type=jnp.float32)
             if k == 0:
@@ -325,46 +365,55 @@
     outer, inner = grid_of(req_size)
     planes = 2 * inner
     tokens = home_cache.shape[0] * home_cache.shape[1]
+    smem = pl.BlockSpec(memory_space=pltpu.SMEM)
     vmem = pl.BlockSpec(memory_space=pltpu.VMEM)
     hbm = pl.BlockSpec(memory_space=pltpu.HBM)
     bf16, f32 = jnp.bfloat16, jnp.float32
     dma = pltpu.SemaphoreType.DMA
-    ints = (home_table.T, home_len, parents, prompt_place, owned_request, prompt_len)
+    singles = (prompt_place, owned_request, prompt_len)
+    ints = (home_table.T, home_len, parents)
     floats = (
         queries.reshape(rows, lanes),
         token_rows(new_kv),
         residual.reshape(rows, depth),
-        norm_gain.reshape(1, depth),
+        norm_gain.reshape(-1, LANES),
         token_rows(home_cache),
         token_rows(prompt_cache),
         out_weight,
         qkv_weight.transpose(1, 0, 2),
     )
     wide = lanes + LANES
-    sems = [
-        (len(ints) + len(floats),),
-        (outer,), (outer,), (outer,), (outer,), (planes,), (planes,),
-        (outer,), (outer,), (planes,), (planes,),
-        (OUT_CHUNKS * tp_size,), (tp_size, OUT_CHUNKS),
-    ]
+    half = rows // 2
+
+    def route(first, second, width):
+        return [
+            pltpu.VMEM((first, half, width), bf16),
+            pltpu.VMEM((second - 1, half, width), bf16),
+            pltpu.VMEM((second, half, width), bf16),
+        ]
+
+    hops = [outer, planes] + [outer, planes, planes, outer] * 2
+    sems = [(len(ints) + len(floats),), (OUT_CHUNKS * tp_size,), (tp_size, OUT_CHUNKS)]
+    sems += [(size,) for size in hops for _ in range(2)]
     qkv, res = pl.pallas_call(
         functools.partial(kernel, req_size, tp_size, steps),
         out_shape=(
             jax.ShapeDtypeStruct((steps, 3, beams, lanes), bf16),
             jax.ShapeDtypeStruct((rows, depth), bf16),
         ),
-        in_specs=[hbm] * (len(ints) + len(floats)),
+        in_specs=[smem] * len(singles) + [hbm] * (len(ints) + len(floats)),
         out_specs=(vmem, vmem),
         scratch_shapes=[pltpu.SMEM(a.shape, jnp.int32) for a in ints]
         + [pltpu.VMEM(a.shape, bf16) for a in floats]
         + [
             pltpu.VMEM((outer, 16, LANES), bf16),
-            pltpu.VMEM((outer, rows, lanes), bf16),
-            pltpu.VMEM((planes - 1, rows, lanes), bf16),
-            pltpu.VMEM((planes, rows, lanes), bf16),
-            pltpu.VMEM((outer, rows, wide), bf16),
-            pltpu.VMEM((planes - 1, rows, wide), bf16),
-            pltpu.VMEM((planes, rows, wide), bf16),
+            pltpu.VMEM((planes, 16, LANES), bf16),
+        ]
+        + route(outer, planes, lanes)
+        + route(planes, outer, lanes)
+        + route(outer, planes, wide)
+        + route(planes, outer, wide)
+        + [
             pltpu.VMEM((tp_size, OUT_CHUNKS, rows, depth // OUT_CHUNKS), bf16),
             pltpu.VMEM((rows, lanes), bf16),
             pltpu.VMEM((rows, lanes), bf16),
@@ -377,9 +426,9 @@
         ]
         + [dma(shape) for shape in sems],
         compiler_params=pltpu.CompilerParams(
-            collective_id=0, has_side_effects=True, vmem_limit_bytes=56 * 1024 * 1024
+            collective_id=0, has_side_effects=True, vmem_limit_bytes=40 * 1024 * 1024
         ),
-    )(*ints, *floats)
+    )(*singles, *(pltpu.with_memory_space_constraint(x, pltpu.HBM) for x in ints + floats))
     return qkv.transpose(0, 2, 1, 3), res.reshape(steps, beams, depth)
 
 

time: 37 us -> 30.6 us (0.83)
  Pallas kernels: 29.8 us -> 26.6 us
  local copies, waits for them, and re-layouts: 4.4 us -> 1.3 us
    pallas_call x1, Pallas kernels: 29.8 us -> 26.6 us  [shards(): pl.pallas_call(functools.partial(kernel, req_size, tp_size, steps), out_s...]
    unnamed x2, local copies, waits for them, and re-layouts: 3.11 us -> 1.3 us
    reshape x1 -> x0, local copies, waits for them, and re-layouts: 1.29 us -> none  [shards(): norm_gain.reshape(1, depth)]
where the time goes in v3:
time: 30.6 us; the launch traced here: 30.5 us
  Pallas kernels  26.6 us (87%)
  between operations  2.58 us (8%)
  local copies, waits for them, and re-layouts  1.3 us (4%)
    pallas_call x1, Pallas kernels, shards(): pl.pallas_call(functools.partial(kernel, req_size, tp_size, steps), out_s...  26.6 us
    unnamed x2, local copies, waits for them, and re-layouts  1.3 us

profile of v3, /device:TPU:0, one launch (start us, length us, event | category | flops | bytes accessed | tf_op | source)
XLA Modules:
  0.0 30.5 jit_solution(8286331273837625410)
XLA Ops:
  2.6 26.6 %shard_map.149 = (bf16[4,3,8,512]{3,2,1,0:T(8,128)(2,1)S(1)}, bf16[32,2048]{1,0:T(8,128)(2,1)S(1)}) custom-call(s32[1]{0:T(128)S(6)} %copy.21.place_ref, s32[1]{0:T(128)S(6)} %copy.22.owned_ref, s32[1]{0:T(128)S(6)} %copy.23.plen_ref, s32[4,8]{1,0:T(4,128)} %bitcast.31, s32[8]{0:T(128)} %len_any.1, s32[4,8]{1,0:T(4,128)} %parents_any.1, ...), custom_call_target="tpu_custom_call" | custom-call | tf_op jit(solution)/shard_map/pallas_call | solution.py:398
  29.2 0.6 %copy.24 = bf16[4,8,3,512]{3,1,2,0:T(8,128)(2,1)} copy(bf16[4,8,3,512]{3,1,2,0:T(8,128)(2,1)S(1)} %bitcast.23) | data formatting | bytes 196608
  29.8 0.7 %copy.25 = bf16[4,8,2048]{2,1,0:T(8,128)(2,1)} copy(bf16[4,8,2048]{2,1,0:T(8,128)(2,1)S(1)} %bitcast.22) | data formatting | bytes 262144

commit v4 on v3

--- a/solution.py
+++ b/solution.py
@@ -202,7 +202,8 @@
     first_hop(qb, plane, qb_sem)
     first_hop(meta_c, column, meta_c_sem)
     first_hop(qa, column, qa_sem)
-    pool_count, new_count = key_counts()
+    loads[4].wait()
+    split_blocks(prompt_raw, pk, pv)
 
     def marks_of(meta):
         rows_of = [meta[s].astype(jnp.float32) for s in range(meta.shape[0])]
@@ -213,8 +214,6 @@
     places_p, owners_p = marks_of(meta_p)
     wait_hop(qb, plane, qb_sem)
     second_hop(qb, places_p, qb_msg, qb_in, column, qb2_sem)
-    loads[4].wait()
-    split_blocks(prompt_raw, pk, pv)
     wait_hop(meta_c, column, meta_c_sem)
     places_c, owners_c = marks_of(meta_c)
     wait_hop(qa, column, qa_sem)
@@ -226,6 +225,15 @@
     wait_hop(qa_in, plane, qa2_sem)
     wait_hop(qb_in, column, qb2_sem)
 
+    stat_lane = lax.broadcasted_iota(jnp.int32, (rows, LANES), 1)
+    head_lane = stat_lane < heads
+
+    def by_lane(values):
+        packed = jnp.zeros((rows, LANES), jnp.float32)
+        for h in range(heads):
+            packed = jnp.where(stat_lane == h, values[h * rows : (h + 1) * rows], packed)
+        return packed
+
     owned = owned_ref[0]
     asked = jnp.concatenate([qa_in[lax.rem(owned, planes)], qb_in[owned // planes]], axis=0)
     asked = spread_heads(asked, heads)
@@ -236,19 +244,18 @@
     weights = jnp.exp(scores - top).astype(jnp.bfloat16)
     total = jnp.sum(weights.astype(jnp.float32), axis=1, keepdims=True)
     wide = jnp.dot(weights, pv[...], preferred_element_type=jnp.float32)
+    total = by_lane(total)
     part_of = 1.0 / total
-    log_total = top + jnp.log(total)
-    stat_lane = lax.broadcasted_iota(jnp.int32, (rows, LANES), 1)
+    rest = by_lane(top) + jnp.where(head_lane, jnp.log(total), 0.0)
     stats = jnp.zeros((rows, LANES), jnp.float32)
-    rest = log_total
     for part in range(3):
         level = rest.astype(jnp.bfloat16).astype(jnp.float32)
         rest = rest - level
-        for h in range(heads):
-            stats = jnp.where(stat_lane == part * heads + h, level[h * rows : (h + 1) * rows], stats)
+        stats = stats + (pltpu.roll(level, part * heads, 1) if part else level)
+
     def answer(h, cols):
         own = slice(h * rows, (h + 1) * rows)
-        return wide[own, cols] * part_of[own]
+        return wide[own, cols] * part_of[:, h : h + 1]
 
     answers = own_columns(rows, lanes, answer).astype(jnp.bfloat16)
     stats = stats.astype(jnp.bfloat16)
@@ -258,6 +265,7 @@
     ra[o, :, lanes:] = stats[:half]
     first_hop(rb, plane, rb_sem)
     first_hop(ra, column, ra_sem)
+    pool_count, new_count = key_counts()
 
     wait_hop(rb, plane, rb_sem)
     second_hop(rb, owners_p, rb_msg, rb_in, column, rb2_sem)
@@ -277,6 +285,9 @@
     numer = jnp.dot(pool_w.astype(jnp.bfloat16), hv[...], preferred_element_type=jnp.float32)
     numer = numer + jnp.dot(new_w, nv[...], preferred_element_type=jnp.float32)
 
+    home_top = by_lane(home_top)
+    home_sum = by_lane(home_sum)
+
     wait_hop(ra, column, ra_sem)
     second_hop(ra, owners_c, ra_msg, ra_in, plane, ra2_sem)
     wait_hop(ra_in, plane, ra2_sem)
@@ -285,14 +296,8 @@
     reply = jnp.concatenate([ra_in[lax.rem(place, planes)], rb_in[place // planes]], axis=0)
     reply = reply.astype(jnp.float32)
     stats = reply[:, lanes:]
-    reply_log = []
-    for h in range(heads):
-        reply_log.append(
-            stats[:, h : h + 1]
-            + stats[:, heads + h : heads + h + 1]
-            + stats[:, 2 * heads + h : 2 * heads + h + 1]
-        )
-    reply_log = jnp.concatenate(reply_log, axis=0)
+    reply_log = stats + pltpu.roll(stats, LANES - heads, 1) + pltpu.roll(stats, LANES - 2 * heads, 1)
+    reply_log = jnp.where(head_lane, reply_log, 0.0)
     joint = jnp.maximum(home_top, reply_log)
     home_factor = jnp.exp(home_top - joint)
     prompt_factor = jnp.exp(reply_log - joint)
@@ -302,7 +307,8 @@
 
     def joined(h, cols):
         own = slice(h * rows, (h + 1) * rows)
-        return numer[own, cols] * home_factor[own] + reply[:, cols] * prompt_factor[own]
+        lane = slice(h, h + 1)
+        return numer[own, cols] * home_factor[:, lane] + reply[:, cols] * prompt_factor[:, lane]
 
     attended = own_columns(rows, lanes, joined).astype(jnp.bfloat16)
 
@@ -345,6 +351,17 @@
 
     for copy in sent:
         copy.wait_send()
+
+
+def store(qkv_ref, res_ref, qkv_out, res_out, sems):
+    copies = [
+        pltpu.make_async_copy(qkv_ref, qkv_out, sems.at[0]),
+        pltpu.make_async_copy(res_ref, res_out, sems.at[1]),
+    ]
+    for copy in copies:
+        copy.start()
+    for copy in copies:
+        copy.wait()
 
 
 def token_rows(cache):
@@ -429,6 +446,16 @@
             collective_id=0, has_side_effects=True, vmem_limit_bytes=40 * 1024 * 1024
         ),
     )(*singles, *(pltpu.with_memory_space_constraint(x, pltpu.HBM) for x in ints + floats))
+    qkv, res = pl.pallas_call(
+        store,
+        out_shape=(
+            jax.ShapeDtypeStruct(qkv.shape, bf16),
+            jax.ShapeDtypeStruct(res.shape, bf16),
+        ),
+        in_specs=[vmem, vmem],
+        out_specs=(hbm, hbm),
+        scratch_shapes=[dma((2,))],
+    )(qkv, res)
     return qkv.transpose(0, 2, 1, 3), res.reshape(steps, beams, depth)
 
 

time: 30.6 us -> 32.3 us (1.056)
  Pallas kernels: 26.6 us -> 28.3 us
    pallas_call x0 -> x1, Pallas kernels: none -> 1.65 us  [shards(): pl.pallas_call(store, out_shape=(jax.ShapeDtypeStruct(qkv.shape, bf16), j...]
    unnamed x2 -> x4, local copies, waits for them, and re-layouts: 1.3 us -> 1.27 us
where the time goes in v4:
time: 32.3 us; the launch traced here: 32.1 us
  Pallas kernels  28.3 us (88%)
  between operations  2.59 us (8%)
  local copies, waits for them, and re-layouts  1.27 us (4%)
    pallas_call x1, Pallas kernels, shards(): pl.pallas_call(functools.partial(kernel, req_size, tp_size, steps), out_s...  26.6 us
    pallas_call x1, Pallas kernels, shards(): pl.pallas_call(store, out_shape=(jax.ShapeDtypeStruct(qkv.shape, bf16), j...  1.65 us
    unnamed x4, local copies, waits for them, and re-layouts  1.27 us

profile of v4, /device:TPU:0, one launch (start us, length us, event | category | flops | bytes accessed | tf_op | source)
XLA Modules:
  0.0 32.1 jit_solution(858839237503811780)
XLA Ops:
  2.6 26.6 %shard_map.149 = (bf16[4,3,8,512]{3,2,1,0:T(8,128)(2,1)S(1)}, bf16[32,2048]{1,0:T(8,128)(2,1)S(1)}) custom-call(s32[1]{0:T(128)S(6)} %copy.19.place_ref, s32[1]{0:T(128)S(6)} %copy.20.owned_ref, s32[1]{0:T(128)S(6)} %copy.21.plen_ref, s32[4,8]{1,0:T(4,128)} %bitcast.29, s32[8]{0:T(128)} %len_any.1, s32[4,8]{1,0:T(4,128)} %parents_any.1, ...), custom_call_target="tpu_custom_call" | custom-call | tf_op jit(solution)/shard_map/pallas_call | solution.py:415
  29.2 0.0 copy-start
  29.2 0.6 %copy-done = bf16[32,2048]{1,0:T(8,128)(2,1)} copy-done((bf16[32,2048]{1,0:T(8,128)(2,1)}, bf16[32,2048]{1,0:T(8,128)(2,1)S(1)}, u32[]{:S(2)}) %copy-start) | copy-done | bytes 131096
  29.9 0.0 copy-start.1
  29.9 0.6 %copy-done.1 = bf16[4,3,8,512]{3,2,1,0:T(8,128)(2,1)} copy-done((bf16[4,3,8,512]{3,2,1,0:T(8,128)(2,1)}, bf16[4,3,8,512]{3,2,1,0:T(8,128)(2,1)S(1)}, u32[]{:S(2)}) %copy-start.1) | copy-done | bytes 98328
  30.5 1.7 %shard_map.150 = (bf16[4,3,8,512]{3,2,1,0:T(8,128)(2,1)}, bf16[32,2048]{1,0:T(8,128)(2,1)}) custom-call(bf16[4,3,8,512]{3,2,1,0:T(8,128)(2,1)} %copy-done.1, bf16[32,2048]{1,0:T(8,128)(2,1)} %copy-done), custom_call_target="tpu_custom_call" | custom-call | tf_op jit(solution)/shard_map/pallas_call | solution.py:449
Async XLA Ops:
  29.2 0.6 %copy-start = (bf16[32,2048]{1,0:T(8,128)(2,1)}, bf16[32,2048]{1,0:T(8,128)(2,1)S(1)}, u32[]{:S(2)}) copy-start(bf16[32,2048]{1,0:T(8,128)(2,1)S(1)} %get-tuple-element.7.res_ref) | copy-start | bytes 393220
  29.9 0.6 %copy-start.1 = (bf16[4,3,8,512]{3,2,1,0:T(8,128)(2,1)}, bf16[4,3,8,512]{3,2,1,0:T(8,128)(2,1)S(1)}, u32[]{:S(2)}) copy-start(bf16[4,3,8,512]{3,2,1,0:T(8,128)(2,1)S(1)} %get-tuple-element.6.qkv_ref) | copy-start | bytes 294916

commit v5 on v4

--- a/solution.py
+++ b/solution.py
@@ -115,7 +115,7 @@
         (wo_any, wo), (res_any, res_ref), (gain_any, gain_ref), (wq_any, wq),
     ]
     loads = [pltpu.make_async_copy(src, dst, load_sem.at[n]) for n, (src, dst) in enumerate(pairs)]
-    for copy in loads:
+    for copy in loads[:5]:
         copy.start()
     sent = []
 
@@ -198,10 +198,12 @@
     qa[o] = q_ref[:half, :]
     qb[p] = q_ref[half:, :]
     pl.semaphore_wait(barrier, outer - 1 + planes - 1 + len(tp_peers))
+    first_hop(qa, column, qa_sem)
+    first_hop(qb, plane, qb_sem)
     first_hop(meta_p, plane, meta_p_sem)
-    first_hop(qb, plane, qb_sem)
     first_hop(meta_c, column, meta_c_sem)
-    first_hop(qa, column, qa_sem)
+    loads[5].start()
+    loads[6].start()
     loads[4].wait()
     split_blocks(prompt_raw, pk, pv)
 
@@ -218,6 +220,8 @@
     places_c, owners_c = marks_of(meta_c)
     wait_hop(qa, column, qa_sem)
     second_hop(qa, places_c, qa_msg, qa_in, plane, qa2_sem)
+    for copy in loads[7:]:
+        copy.start()
     loads[5].wait()
     loads[6].wait()
     split_blocks(home_raw, hk, hv)
@@ -259,12 +263,12 @@
 
     answers = own_columns(rows, lanes, answer).astype(jnp.bfloat16)
     stats = stats.astype(jnp.bfloat16)
+    ra[o, :, :lanes] = answers[:half]
+    ra[o, :, lanes:] = stats[:half]
     rb[p, :, :lanes] = answers[half:]
     rb[p, :, lanes:] = stats[half:]
-    ra[o, :, :lanes] = answers[:half]
-    ra[o, :, lanes:] = stats[:half]
+    first_hop(ra, column, ra_sem)
     first_hop(rb, plane, rb_sem)
-    first_hop(ra, column, ra_sem)
     pool_count, new_count = key_counts()
 
     wait_hop(rb, plane, rb_sem)
@@ -351,17 +355,6 @@
 
     for copy in sent:
         copy.wait_send()
-
-
-def store(qkv_ref, res_ref, qkv_out, res_out, sems):
-    copies = [
-        pltpu.make_async_copy(qkv_ref, qkv_out, sems.at[0]),
-        pltpu.make_async_copy(res_ref, res_out, sems.at[1]),
-    ]
-    for copy in copies:
-        copy.start()
-    for copy in copies:
-        copy.wait()
 
 
 def token_rows(cache):
@@ -446,16 +439,6 @@
             collective_id=0, has_side_effects=True, vmem_limit_bytes=40 * 1024 * 1024
         ),
     )(*singles, *(pltpu.with_memory_space_constraint(x, pltpu.HBM) for x in ints + floats))
-    qkv, res = pl.pallas_call(
-        store,
-        out_shape=(
-            jax.ShapeDtypeStruct(qkv.shape, bf16),
-            jax.ShapeDtypeStruct(res.shape, bf16),
-        ),
-        in_specs=[vmem, vmem],
-        out_specs=(hbm, hbm),
-        scratch_shapes=[dma((2,))],
-    )(qkv, res)
     return qkv.transpose(0, 2, 1, 3), res.reshape(steps, beams, depth)
 
 

time: 32.3 us -> 30.7 us (0.950)
  Pallas kernels: 28.3 us -> 26.7 us
    pallas_call x1 -> x0, Pallas kernels: 1.65 us -> none  [shards(): pl.pallas_call(store, out_shape=(jax.ShapeDtypeStruct(qkv.shape, bf16), j...]
    unnamed x4 -> x2, local copies, waits for them, and re-layouts: 1.27 us -> 1.3 us
where the time goes in v5:
time: 30.7 us; the launch traced here: 30.6 us
  Pallas kernels  26.7 us (87%)
  between operations  2.58 us (8%)
  local copies, waits for them, and re-layouts  1.3 us (4%)
    pallas_call x1, Pallas kernels, shards(): pl.pallas_call(functools.partial(kernel, req_size, tp_size, steps), out_s...  26.7 us
    unnamed x2, local copies, waits for them, and re-layouts  1.3 us

profile of v5, /device:TPU:0, one launch (start us, length us, event | category | flops | bytes accessed | tf_op | source)
XLA Modules:
  0.0 30.6 jit_solution(7215550728833260858)
XLA Ops:
  2.6 26.7 %shard_map.149 = (bf16[4,3,8,512]{3,2,1,0:T(8,128)(2,1)S(1)}, bf16[32,2048]{1,0:T(8,128)(2,1)S(1)}) custom-call(s32[1]{0:T(128)S(6)} %copy.21.place_ref, s32[1]{0:T(128)S(6)} %copy.22.owned_ref, s32[1]{0:T(128)S(6)} %copy.23.plen_ref, s32[4,8]{1,0:T(4,128)} %bitcast.31, s32[8]{0:T(128)} %len_any.1, s32[4,8]{1,0:T(4,128)} %parents_any.1, ...), custom_call_target="tpu_custom_call" | custom-call | tf_op jit(solution)/shard_map/pallas_call | solution.py:408
  29.3 0.6 %copy.24 = bf16[4,8,3,512]{3,1,2,0:T(8,128)(2,1)} copy(bf16[4,8,3,512]{3,1,2,0:T(8,128)(2,1)S(1)} %bitcast.23) | data formatting | bytes 196608
  29.9 0.7 %copy.25 = bf16[4,8,2048]{2,1,0:T(8,128)(2,1)} copy(bf16[4,8,2048]{2,1,0:T(8,128)(2,1)S(1)} %bitcast.22) | data formatting | bytes 262144

commit v6 on v5

--- a/solution.py
+++ b/solution.py
@@ -53,15 +53,20 @@
     in_row = lax.broadcasted_iota(jnp.int32, (size, size), 1)
     wanted = (out_row % SPLIT) * kinds + out_row // SPLIT
     order = jnp.where(in_row == wanted, 1.0, 0.0).astype(jnp.bfloat16)
-    for n in range(tokens // SPLIT):
-        sorted_rows = jnp.dot(
-            order, raw[n * size : (n + 1) * size, :], preferred_element_type=jnp.float32
-        ).astype(jnp.bfloat16)
-        for t in range(lanes // LANES):
-            at = 2 * t * SPLIT
-            rows, cols = slice(n * SPLIT, (n + 1) * SPLIT), slice(t * LANES, (t + 1) * LANES)
-            keys[rows, cols] = sorted_rows[at : at + SPLIT]
-            values[rows, cols] = sorted_rows[at + SPLIT : at + 2 * SPLIT]
+    blocks = tokens // SPLIT
+    group = min(4, blocks)
+    for first in range(0, blocks, group):
+        taken = range(first, first + group)
+        beside = [raw[n * size : (n + 1) * size, :] for n in taken]
+        beside = beside[0] if group == 1 else jnp.concatenate(beside, axis=1)
+        ordered = jnp.dot(order, beside, preferred_element_type=jnp.float32).astype(jnp.bfloat16)
+        for g, n in enumerate(taken):
+            rows, own = slice(n * SPLIT, (n + 1) * SPLIT), slice(g * LANES, (g + 1) * LANES)
+            for t in range(lanes // LANES):
+                at = 2 * t * SPLIT
+                cols = slice(t * LANES, (t + 1) * LANES)
+                keys[rows, cols] = ordered[at : at + SPLIT, own]
+                values[rows, cols] = ordered[at + SPLIT : at + 2 * SPLIT, own]
 
 
 def kernel(
@@ -167,23 +172,24 @@
                 live = (lane_block == table_ref[j, b]) & (lane_pos + j * block < len_ref[b])
                 total = total + jnp.where(live, 1.0, 0.0)
             base[b : b + 1, :] = total
-        pool = base[...]
         row8 = lax.broadcasted_iota(jnp.int32, (BEAMS, BEAMS), 0)
         col8 = lax.broadcasted_iota(jnp.int32, (BEAMS, BEAMS), 1)
-        new_row = lax.broadcasted_iota(jnp.int32, (BEAMS, rows), 0)
-        new_col = lax.broadcasted_iota(jnp.int32, (BEAMS, rows), 1)
-        new = jnp.zeros((BEAMS, rows), jnp.float32)
-        pools, news = [], []
+        new_row = lax.broadcasted_iota(jnp.int32, (BEAMS, LANES), 0)
+        new_col = lax.broadcasted_iota(jnp.int32, (BEAMS, LANES), 1)
+        state = jnp.concatenate([base[...], jnp.zeros((BEAMS, LANES), jnp.float32)], axis=1)
+        found = []
         for s in range(steps):
             pick = jnp.zeros((BEAMS, BEAMS), jnp.float32)
             for b in range(BEAMS):
                 pick = jnp.where((row8 == b) & (col8 == parents_ref[s, b]), 1.0, pick)
-            pool = jnp.dot(pick, pool, preferred_element_type=jnp.float32)
-            new = jnp.dot(pick, new, preferred_element_type=jnp.float32)
-            new = new + jnp.where(new_col == new_row + s * BEAMS, 1.0, 0.0)
-            pools.append(pool)
-            news.append(new)
-        return jnp.concatenate(pools, axis=0), jnp.concatenate(news, axis=0)
+            state = jnp.dot(
+                pick.astype(jnp.bfloat16), state.astype(jnp.bfloat16), preferred_element_type=jnp.float32
+            )
+            own = jnp.where(new_col == new_row + s * BEAMS, 1.0, 0.0)
+            state = jnp.concatenate([state[:, :tokens], state[:, tokens:] + own], axis=1)
+            found.append(state)
+        found = jnp.concatenate(found, axis=0)
+        return found[:, :tokens], found[:, tokens : tokens + rows]
 
     for copy in loads[:4]:
         copy.wait()

time: 30.7 us -> 30.7 us (level)
  no operation moved by 1% of the time
where the time goes in v6:
time: 30.7 us; the launch traced here: 30.5 us
  Pallas kernels  26.7 us (87%)
  between operations  2.58 us (8%)
  local copies, waits for them, and re-layouts  1.3 us (4%)
    pallas_call x1, Pallas kernels, shards(): pl.pallas_call(functools.partial(kernel, req_size, tp_size, steps), out_s...  26.7 us
    unnamed x2, local copies, waits for them, and re-layouts  1.3 us

profile of v6, /device:TPU:0, one launch (start us, length us, event | category | flops | bytes accessed | tf_op | source)
XLA Modules:
  0.0 30.5 jit_solution(6212526273508772711)
XLA Ops:
  2.6 26.7 %shard_map.149 = (bf16[4,3,8,512]{3,2,1,0:T(8,128)(2,1)S(1)}, bf16[32,2048]{1,0:T(8,128)(2,1)S(1)}) custom-call(s32[1]{0:T(128)S(6)} %copy.21.place_ref, s32[1]{0:T(128)S(6)} %copy.22.owned_ref, s32[1]{0:T(128)S(6)} %copy.23.plen_ref, s32[4,8]{1,0:T(4,128)} %bitcast.31, s32[8]{0:T(128)} %len_any.1, s32[4,8]{1,0:T(4,128)} %parents_any.1, ...), custom_call_target="tpu_custom_call" | custom-call | tf_op jit(solution)/shard_map/pallas_call | solution.py:414
  29.3 0.6 %copy.24 = bf16[4,8,3,512]{3,1,2,0:T(8,128)(2,1)} copy(bf16[4,8,3,512]{3,1,2,0:T(8,128)(2,1)S(1)} %bitcast.23) | data formatting | bytes 196608
  29.9 0.7 %copy.25 = bf16[4,8,2048]{2,1,0:T(8,128)(2,1)} copy(bf16[4,8,2048]{2,1,0:T(8,128)(2,1)S(1)} %bitcast.22) | data formatting | bytes 262144

commit v7 on v6

--- a/solution.py
+++ b/solution.py
@@ -11,7 +11,7 @@
 HEAD_DIM = 64
 BEAMS = 8
 LANES = 128
-OUT_CHUNKS = 4
+OUT_CHUNKS = 8
 SPLIT = 32
 
 NEG_FILL = -1e30

time: 30.7 us -> 30.7 us (level)
  no operation moved by 1% of the time
where the time goes in v7:
time: 30.7 us; the launch traced here: 30.6 us
  Pallas kernels  26.7 us (87%)
  between operations  2.58 us (8%)
  local copies, waits for them, and re-layouts  1.3 us (4%)
    pallas_call x1, Pallas kernels, shards(): pl.pallas_call(functools.partial(kernel, req_size, tp_size, steps), out_s...  26.7 us
    unnamed x2, local copies, waits for them, and re-layouts  1.3 us

profile of v7, /device:TPU:0, one launch (start us, length us, event | category | flops | bytes accessed | tf_op | source)
XLA Modules:
  0.0 30.6 jit_solution(18256321331854422003)
XLA Ops:
  2.6 26.7 %shard_map.149 = (bf16[4,3,8,512]{3,2,1,0:T(8,128)(2,1)S(1)}, bf16[32,2048]{1,0:T(8,128)(2,1)S(1)}) custom-call(s32[1]{0:T(128)S(6)} %copy.21.place_ref, s32[1]{0:T(128)S(6)} %copy.22.owned_ref, s32[1]{0:T(128)S(6)} %copy.23.plen_ref, s32[4,8]{1,0:T(4,128)} %bitcast.31, s32[8]{0:T(128)} %len_any.1, s32[4,8]{1,0:T(4,128)} %parents_any.1, ...), custom_call_target="tpu_custom_call" | custom-call | tf_op jit(solution)/shard_map/pallas_call | solution.py:414
  29.3 0.6 %copy.24 = bf16[4,8,3,512]{3,1,2,0:T(8,128)(2,1)} copy(bf16[4,8,3,512]{3,1,2,0:T(8,128)(2,1)S(1)} %bitcast.23) | data formatting | bytes 196608
  29.9 0.7 %copy.25 = bf16[4,8,2048]{2,1,0:T(8,128)(2,1)} copy(bf16[4,8,2048]{2,1,0:T(8,128)(2,1)S(1)} %bitcast.22) | data formatting | bytes 262144
